TPU v7x, 128 devices: a whole 4x4x4 slice. The times are simulated.
128 devices in a mesh: client: 4 (over y_hi, core), mp: 32 (over x, z, y_lo).
Axes of the slice: x: 4, y: 4 (y_hi: 2, y_lo: 2; y = y_hi * 2 + y_lo), z: 4, core: 2. Of those that a mesh axis runs over, the one named last changes fastest.
Arguments:
- tokens: bfloat16 [5120, 4096], P(('client', 'mp')), may hold values from -6 to 6
- out_grad: bfloat16 [5120, 4096], P(('client', 'mp'))
- gate_weight: bfloat16 [4096, 14336], P(None, 'mp')
- up_weight: bfloat16 [4096, 14336], P('client', 'mp'), may hold values from -0.09375 to 0.09375
- down_weight: bfloat16 [4096, 14336], P('client', 'mp'), may hold values from -0.046875 to 0.046875
- counts: int32 [4], replicated, may hold values from 1 to 999
- noise: bfloat16 [2, 4096, 14336], P(None, 'client', 'mp'), may hold values from -3 to 3
- first_moment: float32 [2, 4096, 14336], P(None, 'client', 'mp'), may hold values from -2 to 2
- second_moment: float32 [2, 4096, 14336], P(None, 'client', 'mp'), may hold values from 0.01 to 1
Outputs:
- new_first: float32 [2, 4096, 14336], P(None, 'client', 'mp')
- new_second: float32 [2, 4096, 14336], P(None, 'client', 'mp')
- server_step: float32 [2, 4096, 14336], P(None, 'client', 'mp')
All inputs are finite; a program needn't handle non-finite values.
Results may differ from a plain program's by a relative error of at most 0.0019.
Values may be sent and summed in bfloat16 or wider, within the bound.
No kernel may reach another device: no remote copies, remote signals or barrier semaphores. Data moves between devices by JAX's collectives and lax.ppermute only.
A program may use at most 512 MiB of HBM per device.

v0:
```python
import math

import jax
import jax.numpy as jnp
from jax import lax
from jax.experimental import pallas as pl
from jax.experimental.pallas import tpu as pltpu
from jax.sharding import PartitionSpec as P

NX, NZ, NY = 4, 4, 2
BF16, F32 = jnp.bfloat16, jnp.float32
CORNER = (slice(0, 8), slice(0, 128))


def place(x, z, y):
    return (x % NX) * (NZ * NY) + (z % NZ) * NY + y % NY


def pairs(to):
    return [(place(x, z, y), place(*to(x, z, y))) for x in range(NX) for z in range(NZ) for y in range(NY)]


def send(value, dx=0, dz=0, dy=0):
    return lax.ppermute(value, "mp", pairs(lambda x, z, y: (x + dx, z + dz, y + dy)))


def flip(value, bx=0, bz=0, by=0):
    return lax.ppermute(value, "mp", pairs(lambda x, z, y: (x ^ bx, z ^ bz, y ^ by)))


def swap_core(value):
    return lax.ppermute(value, "client", [(c, c ^ 1) for c in range(4)])


def swap_far(value):
    return lax.ppermute(value, "client", [(c, c ^ 2) for c in range(4)])


def token(*others):
    corners = sum(jnp.abs(other[:8, :128].astype(F32)) for other in others)
    return swap_core(swap_core(jnp.minimum(corners, 0.0)))


def held(value, zeros):
    return value.at[:16, :128].add(jnp.concatenate([zeros, zeros]).astype(value.dtype))


def last_zeros(line):
    quarter = line.shape[0] // 4
    ends = [jnp.abs(line[at : at + 8, :128].astype(F32)) for at in (3 * quarter, 4 * quarter - 16)]
    return jnp.minimum(ends[0] + ends[1], 0.0)


def ring(block, axis):
    half = block.shape[0] // 2
    below = send(block, **{axis: 1})
    above = send(block, **{axis: -1})
    return [block, below, above, below[:half], above[half:]]


def far_block(low, high, axis):
    return jnp.concatenate([send(low, **{axis: 1}), send(high, **{axis: -1})], axis=0)


def line_of(own, axis):
    *blocks, low, high = ring(jnp.concatenate([own, send(own, dy=1)], axis=0), axis)
    return jnp.concatenate([*blocks, far_block(low, high, axis)], axis=0)


def rows_dot(rows, weight):
    return lax.dot_general(rows, weight, (((1,), (0,)), ((), ())), preferred_element_type=F32)


def activations(gates, ups, backs, cut):
    flat = [a for group in zip(gates, ups, backs) for a in group]
    units = flat[0].shape[1]
    rows = sum(a.shape[0] for a in gates)

    def kernel(*refs):
        ins, (up_input, hidden) = refs[: len(flat)], refs[len(flat) :]
        for i in range(4):
            for j in range(4):
                here, there = slice(j * cut, (j + 1) * cut), slice(i * cut, (i + 1) * cut)
                gate = ins[3 * i][here, :]
                silu = gate / (1.0 + jnp.exp(-gate))
                up_input[(4 * i + j) * cut : (4 * i + j + 1) * cut, :] = (ins[3 * j + 2][there, :] * silu).astype(BF16)
                hidden[(4 * j + i) * cut : (4 * j + i + 1) * cut, :] = (silu * ins[3 * i + 1][here, :]).astype(BF16)

    whole = pl.BlockSpec(memory_space=pltpu.VMEM)
    return pl.pallas_call(
        kernel,
        in_specs=[whole] * len(flat),
        out_specs=[whole] * 2,
        out_shape=[jax.ShapeDtypeStruct((rows, units), BF16)] * 2,
        compiler_params=pltpu.CompilerParams(vmem_limit_bytes=24 * 2**20),
        cost_estimate=pl.CostEstimate(flops=10 * rows * units, bytes_accessed=16 * rows * units, transcendentals=rows * units),
    )(*flat)


def deltas(xs, ys, up_input, hidden, columns, width, block=512):
    count, units, rows = len(xs), up_input.shape[1], up_input.shape[0]

    def kernel(_, *refs):
        x, y = refs[:count], refs[count : 2 * count]
        up_ref, hidden_ref, up_out, down_out, squares = refs[2 * count :]

        @pl.when((pl.program_id(0) == 0) & (pl.program_id(1) == 0))
        def _():
            squares[...] = jnp.zeros_like(squares)

        for left, pieces, out in ((up_ref, x, up_out), (hidden_ref, y, down_out)):
            right = jnp.concatenate([piece[...] for piece in pieces], axis=0)
            value = lax.dot_general(left[...], right, (((0,), (0,)), ((), ())), preferred_element_type=F32)
            out[0] = value
            folded = (value * value).reshape(units // 8, 8, block).sum(axis=0)
            squares[...] += sum(folded[:, 128 * i : 128 * (i + 1)] for i in range(block // 128))

    per = width // block
    read = lambda i, j, at: (0, at[i] * per + j)
    fixed = lambda i, j, at: (0, 0)
    return pl.pallas_call(
        kernel,
        grid_spec=pltpu.PrefetchScalarGridSpec(
            num_scalar_prefetch=1,
            grid=(2, per),
            in_specs=[pl.BlockSpec((p.shape[0], block), read) for p in (*xs, *ys)]
            + [pl.BlockSpec((rows, units), fixed)] * 2,
            out_specs=[pl.BlockSpec((1, units, block), lambda i, j, at: (i, 0, j))] * 2
            + [pl.BlockSpec((8, 128), fixed)],
        ),
        out_shape=[jax.ShapeDtypeStruct((2, units, width), F32)] * 2 + [jax.ShapeDtypeStruct((8, 128), F32)],
        compiler_params=pltpu.CompilerParams(vmem_limit_bytes=40 * 2**20),
        cost_estimate=pl.CostEstimate(
            flops=8 * rows * units * width, bytes_accessed=8 * rows * width + 16 * units * width, transcendentals=0
        ),
    )(columns, *xs, *ys, up_input, hidden)


def adam(index, row, factors, keep, received, arrived, noise, first, second, outs, block=64):
    units, width = arrived.shape
    base = row // block

    def kernel(factors, keep, received, arrived, noise, first, second, *refs):
        new_first, new_second, step = refs[-3:]
        average = noise[0].astype(F32) + (
            (factors[0] * keep[0] + factors[1] * received[0]) + arrived[...] * factors[2]
        )
        moment = 0.9 * first[0] + 0.1 * average
        spread = 0.99 * second[0] + 0.01 * average * average
        new_first[0] = moment
        new_second[0] = spread
        step[0] = moment / (jnp.sqrt(spread) + 0.001)

    zero = pl.BlockSpec((1, block, width), lambda i: (0, base + i, 0))
    mine = pl.BlockSpec((1, block, width), lambda i: (index, base + i, 0))
    given = () if outs is None else tuple(outs)
    return pl.pallas_call(
        kernel,
        grid=(units // block,),
        in_specs=[
            pl.BlockSpec(memory_space=pltpu.SMEM),
            zero,
            zero,
            pl.BlockSpec((block, width), lambda i: (i, 0)),
            mine,
            mine,
            mine,
        ]
        + [pl.BlockSpec(memory_space=pl.ANY)] * len(given),
        out_specs=[mine] * 3,
        out_shape=[jax.ShapeDtypeStruct(first.shape, F32)] * 3,
        input_output_aliases={7 + i: i for i in range(len(given))},
        compiler_params=pltpu.CompilerParams(vmem_limit_bytes=24 * 2**20),
        cost_estimate=pl.CostEstimate(flops=12 * units * width, bytes_accessed=34 * units * width, transcendentals=units * width),
    )(factors, keep, received, arrived, noise, first, second, *given)


def local(tokens, out_grad, gate_weight, up_weight, down_weight, counts, noise, first_moment, second_moment):
    model_width = tokens.shape[1]
    units = gate_weight.shape[1]
    hidden_units = units * lax.axis_size("mp")
    token_count = tokens.shape[0] * lax.axis_size("mp")
    member = lax.axis_index("client")
    core, far = member % 2, member // 2
    width = model_width // 4

    up_all = lax.all_gather(up_weight, "client", axis=0, tiled=True)
    down_all = lax.all_gather(down_weight, "client", axis=0, tiled=True)

    x_line, y_line = line_of(tokens, "dx"), line_of(out_grad, "dz")
    x_line, y_line = held(x_line, last_zeros(y_line)), held(y_line, last_zeros(x_line))
    *xs, x_low, x_high = ring(x_line, "dz")
    *ys, y_low, y_high = ring(y_line, "dx")
    gates, ups = [rows_dot(xs[0], gate_weight)], [rows_dot(xs[0], up_all)]
    x_far, y_far = far_block(x_low, x_high, "dz"), far_block(y_low, y_high, "dx")
    for x in xs[1:]:
        gates.append(rows_dot(x, gate_weight))
        ups.append(rows_dot(x, up_all))
    backs = [rows_dot(y, down_all) for y in ys]
    mark = token(*gates, *ups, *backs)
    x_far, y_far = held(x_far, mark), held(y_far, mark)
    xs.append(x_far)
    ys.append(y_far)
    gates.append(rows_dot(x_far, gate_weight))
    ups.append(rows_dot(x_far, up_all))
    backs.append(rows_dot(y_far, down_all))
    up_input, hidden = activations(gates, ups, backs, 2 * tokens.shape[0])

    here = jnp.stack([2 * far, 2 * (1 - far)])
    up_sent, down_sent, squares = deltas(xs, ys, up_input, hidden, here + (1 - core), width)
    up_received, down_received = swap_core(up_sent), swap_core(down_sent)
    up_kept, down_kept, more = deltas(xs, ys, up_input, hidden, here + core, width)

    client_total = jnp.full((8, 128), jnp.sum(squares + more), F32)
    client_total = client_total + flip(client_total, by=1)
    for axis in ("bx", "bz"):
        others = [flip(client_total, **{axis: b}) for b in (1, 2, 3)]
        client_total = (client_total + others[0]) + (others[1] + others[2])
    other_total = swap_core(client_total)
    clip_bound = math.sqrt(2.0 * model_width * hidden_units * token_count)
    weights = counts.astype(F32)
    shares = weights / jnp.sum(weights)
    norm_own, norm_other = jnp.sqrt(client_total[0, 0]), jnp.sqrt(other_total[0, 0])
    w_own = shares[member] * (clip_bound / jnp.maximum(norm_own, clip_bound))
    w_other = shares[member ^ 1] * (clip_bound / jnp.maximum(norm_other, clip_bound))
    most = w_own * norm_own + w_other * norm_other
    power = 14.0 - jnp.ceil(jnp.log2(jnp.where(most > 0.0, most, 1.0)))
    scale = jnp.exp2(jnp.clip(power, -100.0, 100.0))
    their_scale = swap_far(jnp.full((8, 128), scale, F32))[0, 0]
    factors = jnp.stack([w_own, w_other, 1.0 / their_scale])

    def weighted(kept, received, rows):
        total = (w_own * kept[1, rows] + w_other * received[1, rows]) * scale
        return total.astype(jnp.float16)

    cut = 256
    turn = lambda a: a.transpose(0, 2, 1)
    states = [turn(a) for a in (noise, first_moment, second_moment)]
    up_arrived = swap_far(weighted(up_kept, up_received, slice(None))).astype(F32)
    down_low = swap_far(weighted(down_kept, down_received, slice(0, cut))).astype(F32)
    outs = adam(0, 0, factors, up_kept, up_received, up_arrived, *states, None)
    down_high = weighted(down_kept, down_received, slice(cut, None))
    down_high = swap_far(held(down_high, jnp.minimum(jnp.abs(outs[0][0, :8, :128]), 0.0))).astype(F32)
    outs = adam(1, 0, factors, down_kept, down_received, down_low, *states, outs)
    outs = adam(1, cut, factors, down_kept, down_received, down_high, *states, outs)
    return tuple(turn(a) for a in outs)


def solution(mesh):
    state = P(None, "client", "mp")
    rows = P(("client", "mp"), None)
    placed = (rows, rows, P(None, "mp"), P("client", "mp"), P("client", "mp"), P(), state, state, state)
    return jax.shard_map(local, mesh=mesh, in_specs=placed, out_specs=(state,) * 3, check_vma=False)
```

profile of v0, /device:TPU:0, one launch (start us, length us, event | category | flops | bytes accessed | tf_op | source)
XLA Modules:
  0.0 281.5 jit_solution(15677422133967909873)
XLA Ops:
  7.9 1.7 collective-permute-start
  10.0 1.9 constant_dynamic-update-slice_fusion.1
  11.9 1.7 constant_dynamic-update-slice_fusion.15
  13.7 5.2 %collective-permute-done = bf16[40,4096]{1,0:T(8,128)(2,1)S(1)} collective-permute-done((bf16[40,4096]{1,0:T(8,128)(2,1)}, bf16[40,4096]{1,0:T(8,128)(2,1)S(1)}, u32[]{:S(2)}, u32[]{:S(2)}) %collective-permute-start) | collective-permute-done | bytes 327712 | tf_op jit(solution)/shard_map/ppermute | solution.py:24
  21.3 1.7 collective-permute-start.2
  23.0 3.0 %collective-permute-done.5 = bf16[40,4096]{1,0:T(8,128)(2,1)S(1)} collective-permute-done((bf16[40,4096]{1,0:T(8,128)(2,1)}, bf16[40,4096]{1,0:T(8,128)(2,1)S(1)}, u32[]{:S(2)}, u32[]{:S(2)}) %collective-permute-start.5) | collective-permute-done | bytes 327712 | tf_op jit(solution)/shard_map/ppermute | solution.py:24
  26.8 2.1 collective-permute-start.6
  28.9 2.9 %collective-permute-start.8 = (bf16[80,4096]{1,0:T(8,128)(2,1)}, bf16[80,4096]{1,0:T(8,128)(2,1)}, u32[]{:S(2)}, u32[]{:S(2)}) collective-permute-start(bf16[80,4096]{1,0:T(8,128)(2,1)} %get-tuple-element.98), channel_id=1, source_target_pairs={{0,6},{1,7},{2,0},{3,1},{4,2},{5,3},{6,4},{7,5},{8,14},{9,15},{10,... | collective-permute-start | bytes 1966088 | tf_op jit(solution)/shard_map/ppermute | solution.py:24
  31.8 3.7 %collective-permute-done.1 = bf16[80,4096]{1,0:T(8,128)(2,1)S(1)} collective-permute-done((bf16[80,4096]{1,0:T(8,128)(2,1)}, bf16[80,4096]{1,0:T(8,128)(2,1)S(1)}, u32[]{:S(2)}, u32[]{:S(2)}) %collective-permute-start.1) | collective-permute-done | bytes 655392 | tf_op jit(solution)/shard_map/ppermute | solution.py:24
  37.3 2.6 collective-permute-start.4
  39.9 3.9 %collective-permute-done.6 = bf16[80,4096]{1,0:T(8,128)(2,1)} collective-permute-done((bf16[80,4096]{1,0:T(8,128)(2,1)}, bf16[80,4096]{1,0:T(8,128)(2,1)}, u32[]{:S(2)}, u32[]{:S(2)}) %collective-permute-start.6) | collective-permute-done | bytes 655392 | tf_op jit(solution)/shard_map/ppermute | solution.py:24
  45.9 3.3 %collective-permute-start.9 = (bf16[40,4096]{1,0:T(8,128)(2,1)S(1)}, bf16[40,4096]{1,0:T(8,128)(2,1)S(1)}, u32[]{:S(2)}, u32[]{:S(2)}) collective-permute-start(bf16[40,4096]{1,0:T(8,128)(2,1)S(1)} %slice.252), channel_id=1, source_target_pairs={{0,6},{1,7},{2,0},{3,1},{4,2},{5,3},{6,4},{7,5},{8,14},{9,15},{10,... | collective-permute-start | bytes 983048 | tf_op jit(solution)/shard_map/ppermute | solution.py:24
  50.1 2.0 constant_dynamic-update-slice_fusion.4
  57.4 3.2 %collective-permute-start.11 = (bf16[320,4096]{1,0:T(8,128)(2,1)}, bf16[320,4096]{1,0:T(8,128)(2,1)}, u32[]{:S(2)}, u32[]{:S(2)}) collective-permute-start(bf16[320,4096]{1,0:T(8,128)(2,1)} %fusion.24.refs_0_), channel_id=1, source_target_pairs={{0,6},{1,7},{2,0},{3,1},{4,2},{5,3},{6,4},{7,5},{8,14},{9,15},{10,... | collective-permute-start | bytes 7864328 | tf_op jit(solution)/shard_map/ppermute | solution.py:24
  64.9 1.7 collective-permute-start.15
  66.7 4.4 %fusion.28.refs_0_ = f32[320,448]{1,0:T(8,128)S(1)} fusion(bf16[320,4096]{1,0:T(8,128)(2,1)} %fusion.24.refs_0_, bf16[4096,448]{0,1:T(8,128)(2,1)} %param.21), kind=kOutput, calls=%fused_computation.77 | convolution fusion | flops 1174405120 | bytes 6864896 | tf_op jit(solution)/shard_map/dot_general | solution.py:71
  71.1 42.0 %collective-permute-done.10.refs_1_ = bf16[320,4096]{1,0:T(8,128)(2,1)S(1)} collective-permute-done((bf16[320,4096]{1,0:T(8,128)(2,1)}, bf16[320,4096]{1,0:T(8,128)(2,1)S(1)}, u32[]{:S(2)}, u32[]{:S(2)}) %collective-permute-start.10) | collective-permute-done | bytes 2621472 | tf_op jit(solution)/shard_map/ppermute | solution.py:24
  114.5 2.6 slice.255
  117.1 3.2 %collective-permute-start.13 = (bf16[160,4096]{1,0:T(8,128)(2,1)}, bf16[160,4096]{1,0:T(8,128)(2,1)}, u32[]{:S(2)}, u32[]{:S(2)}) collective-permute-start(bf16[160,4096]{1,0:T(8,128)(2,1)} %slice.255), channel_id=1, source_target_pairs={{0,6},{1,7},{2,0},{3,1},{4,2},{5,3},{6,4},{7,5},{8,14},{9,15},{10,... | collective-permute-start | bytes 3932168 | tf_op jit(solution)/shard_map/ppermute | solution.py:24
  120.3 2.5 slice.268
  124.2 2.5 slice.269
  126.7 1.8 collective-permute-start.19
  128.5 2.4 fusion.29.refs_3_
  130.9 4.1 %fusion.30.refs_6_ = f32[320,448]{1,0:T(8,128)} fusion(bf16[320,4096]{1,0:T(8,128)(2,1)} %collective-permute-done.11.refs_2_, bf16[4096,448]{0,1:T(8,128)(2,1)S(1)} %copy-done.14), kind=kOutput, calls=%fused_computation.79 | convolution fusion | flops 1174405120 | bytes 6864896 | tf_op jit(solution)/shard_map/dot_general | solution.py:71
  135.0 4.6 %fusion.32.refs_4_ = f32[320,448]{1,0:T(8,128)} fusion(bf16[320,4096]{1,0:T(8,128)(2,1)S(1)} %collective-permute-done.10.refs_1_, bf16[4096,448]{0,1:T(8,128)(2,1)} %all-gather.3.cloned.1.call-done), kind=kOutput, calls=%fused_computation.81 | convolution fusion | flops 1174405120 | bytes 6864896 | tf_op jit(solution)/shard_map/dot_general | solution.py:71
  139.6 4.1 %fusion.33.refs_7_ = f32[320,448]{1,0:T(8,128)} fusion(bf16[320,4096]{1,0:T(8,128)(2,1)} %collective-permute-done.11.refs_2_, bf16[4096,448]{0,1:T(8,128)(2,1)S(1)} %copy-done.16), kind=kOutput, calls=%fused_computation.82 | convolution fusion | flops 1174405120 | bytes 6864896 | tf_op jit(solution)/shard_map/dot_general | solution.py:71
  143.8 4.5 %fusion.35.refs_5_ = f32[320,448]{1,0:T(8,128)S(1)} fusion(bf16[320,4096]{1,0:T(8,128)(2,1)} %collective-permute-done.14.refs_5_, bf16[4096,448]{0,1:T(8,128)(2,1)} %all-gather.5.cloned.1.call-done), kind=kOutput, calls=%fused_computation.84 | convolution fusion | flops 1174405120 | bytes 6864896 | tf_op jit(solution)/shard_map/dot_general | solution.py:71
  148.3 3.4 %fusion.36.refs_8_ = f32[320,448]{1,0:T(8,128)S(1)} fusion(bf16[320,4096]{1,0:T(8,128)(2,1)} %collective-permute-done.15.refs_6_, bf16[4096,448]{0,1:T(8,128)(2,1)S(1)} %copy-done.18), kind=kOutput, calls=%fused_computation.85 | convolution fusion | flops 1174405120 | bytes 6864896 | tf_op jit(solution)/shard_map/dot_general | solution.py:71
  151.8 3.4 %fusion.31.refs_1_ = f32[320,448]{1,0:T(8,128)S(1)} fusion(bf16[320,4096]{1,0:T(8,128)(2,1)} %fusion.24.refs_0_, bf16[4096,448]{0,1:T(8,128)(2,1)S(1)} %copy-done.17), kind=kOutput, calls=%fused_computation.80 | convolution fusion | flops 1174405120 | bytes 6864896 | tf_op jit(solution)/shard_map/dot_general | solution.py:71
  157.0 2.0 pad_maximum_fusion
  159.8 2.3 pad_maximum_fusion.1
  168.3 9.3 %shard_map.113 = (f32[2,448,1024]{2,1,0:T(8,128)}, f32[2,448,1024]{2,1,0:T(8,128)}, f32[8,128]{1,0:T(8,128)S(1)}) custom-call(s32[2]{0:T(128)S(1)} %get-tuple-element.110._, bf16[320,4096]{1,0:T(8,128)(2,1)} %fusion.24.refs_0_, bf16[320,4096]{1,0:T(8,128)(2,1)S(1)} %collective-permute-done.10.refs_1_, bf16[320,4096]{1,0:T(8,128)(2,1)} %collective-permute-done.11.refs_2_, ...), custom_call_target="tpu_custom_call" | custom-call | flops 4697620480 | bytes 17825792 | tf_op jit(solution)/shard_map/pallas_call | solution.py:121
  178.1 1.7 copy-done.5
  179.8 9.3 %shard_map.114 = (f32[2,448,1024]{2,1,0:T(8,128)}, f32[2,448,1024]{2,1,0:T(8,128)}, f32[8,128]{1,0:T(8,128)S(1)}) custom-call(s32[2]{0:T(128)S(1)} %get-tuple-element.109._, bf16[320,4096]{1,0:T(8,128)(2,1)} %fusion.24.refs_0_, bf16[320,4096]{1,0:T(8,128)(2,1)S(1)} %copy-done.5, bf16[320,4096]{1,0:T(8,128)(2,1)} %collective-permute-done.11.refs_2_, ...), custom_call_target="tpu_custom_call" | custom-call | flops 4697620480 | bytes 17825792 | tf_op jit(solution)/shard_map/pallas_call | solution.py:121
  190.5 2.2 collective-permute-start.20
  195.4 2.7 collective-permute-start.22
  198.1 1.6 collective-permute-start.23
  200.5 2.4 collective-permute-done.23
  205.3 3.1 %collective-permute-start.26 = (f32[8,128]{1,0:T(8,128)S(1)}, f32[8,128]{1,0:T(8,128)S(1)}, u32[]{:S(2)}, u32[]{:S(2)}) collective-permute-start(f32[8,128]{1,0:T(8,128)S(1)} %add_add_fusion.1), channel_id=1, source_target_pairs={{0,6},{1,7},{2,4},{3,5},{4,2},{5,3},{6,0},{7,1},{8,14},{9,15},{10,... | collective-permute-start | bytes 12296 | tf_op jit(solution)/shard_map/ppermute | solution.py:28
  215.2 2.7 fusion.6
  217.9 3.4 %collective-permute-start.31 = (f16[448,1024]{1,0:T(8,128)(2,1)S(1)}, f16[448,1024]{1,0:T(8,128)(2,1)S(1)}, u32[]{:S(2)}, u32[]{:S(2)}) collective-permute-start(f16[448,1024]{1,0:T(8,128)(2,1)S(1)} %fusion.6), channel_id=1, source_target_pairs={{0,64},{32,96},{64,0},{96,32},{1,65},{33,97},{65,1},{97,33},{2,66}... | collective-permute-start | bytes 2752520 | tf_op jit(solution)/shard_map/ppermute | solution.py:36
  221.5 20.9 %collective-permute-done.28 = f32[8,128]{1,0:T(8,128)S(1)} collective-permute-done((f32[8,128]{1,0:T(8,128)S(1)}, f32[8,128]{1,0:T(8,128)S(1)}, u32[]{:S(2)}, u32[]{:S(2)}) %collective-permute-start.28) | collective-permute-done | bytes 4128 | tf_op jit(solution)/shard_map/ppermute | solution.py:36
  245.3 3.3 %collective-permute-start.33 = (f16[256,1024]{1,0:T(8,128)(2,1)S(1)}, f16[256,1024]{1,0:T(8,128)(2,1)S(1)}, u32[]{:S(2)}, u32[]{:S(2)}) collective-permute-start(f16[256,1024]{1,0:T(8,128)(2,1)S(1)} %fusion.10), channel_id=1, source_target_pairs={{0,64},{32,96},{64,0},{96,32},{1,65},{33,97},{65,1},{97,33},{2,66}... | collective-permute-start | bytes 1572872 | tf_op jit(solution)/shard_map/ppermute | solution.py:36
  250.1 2.0 copy-done.6
  252.2 6.2 %shard_map.115 = (f32[2,448,1024]{2,1,0:T(8,128)}, f32[2,448,1024]{2,1,0:T(8,128)}, f32[2,448,1024]{2,1,0:T(8,128)}) custom-call(f32[3]{0:T(128)S(1)} %pad_maximum_fusion.3.factors, f32[2,448,1024]{2,1,0:T(8,128)S(1)} %copy-done.6, f32[2,448,1024]{2,1,0:T(8,128)} %collective-permute-done.30.received, f32[448,1024]{1,0:T(8,128)S(1)} %convert_element_type.56.arrived, ...), custom_call_target="tpu_custom_call" | custom-call | flops 5505024 | bytes 15597568 | tf_op jit(solution)/shard_map/pallas_call | solution.py:157
  260.6 4.0 %shard_map.116 = (f32[2,448,1024]{2,1,0:T(8,128)}, f32[2,448,1024]{2,1,0:T(8,128)}, f32[2,448,1024]{2,1,0:T(8,128)}) custom-call(f32[3]{0:T(128)S(1)} %pad_maximum_fusion.3.factors, f32[2,448,1024]{2,1,0:T(8,128)S(1)} %copy-done.2, f32[2,448,1024]{2,1,0:T(8,128)} %collective-permute-done.29.received, ...), custom_call_target="tpu_custom_call", output_to_operand_aliasing={{0}: (7, {}), {1}: (8, {}), {2}: (9, {})} | custom-call | flops 3145728 | bytes 8912896 | tf_op jit(solution)/shard_map/pallas_call | solution.py:157
  264.6 6.5 %collective-permute-done.32 = f16[192,1024]{1,0:T(8,128)(2,1)S(1)} collective-permute-done((f16[192,1024]{1,0:T(8,128)(2,1)S(1)}, f16[192,1024]{1,0:T(8,128)(2,1)S(1)}, u32[]{:S(2)}, u32[]{:S(2)}) %collective-permute-start.32) | collective-permute-done | bytes 393248 | tf_op jit(solution)/shard_map/ppermute | solution.py:36
  271.2 3.5 %shard_map.117 = (f32[2,448,1024]{2,1,0:T(8,128)}, f32[2,448,1024]{2,1,0:T(8,128)}, f32[2,448,1024]{2,1,0:T(8,128)}) custom-call(f32[3]{0:T(128)S(1)} %pad_maximum_fusion.3.factors, f32[2,448,1024]{2,1,0:T(8,128)S(1)} %copy-done.2, f32[2,448,1024]{2,1,0:T(8,128)} %collective-permute-done.29.received, ...), custom_call_target="tpu_custom_call", output_to_operand_aliasing={{0}: (7, {}), {1}: (8, {}), {2}: (9, {})} | custom-call | flops 2359296 | bytes 6684672 | tf_op jit(solution)/shard_map/pallas_call | solution.py:157
  (134 shorter events, 48.2 us)
Async XLA Ops:
  7.2 127.9 %all-gather.3.cloned.1.call-start = ((), (), s32[]{:S(2)}) async-start(), calls=%async_computation | async-start | bytes 4587520 | tf_op jit(solution)/shard_map/all_gather | solution.py:187
  7.9 135.9 %all-gather.5.cloned.1.call-start = ((), (), s32[]{:S(2)}) async-start(), calls=%async_computation.1 | async-start | bytes 4587520 | tf_op jit(solution)/shard_map/all_gather | solution.py:188
  7.9 10.9 %collective-permute-start = (bf16[40,4096]{1,0:T(8,128)(2,1)}, bf16[40,4096]{1,0:T(8,128)(2,1)S(1)}, u32[]{:S(2)}, u32[]{:S(2)}) collective-permute-start(bf16[40,4096]{1,0:T(8,128)(2,1)} %param.19), channel_id=1, source_target_pairs={{0,1},{1,0},{2,3},{3,2},{4,5},{5,4},{6,7},{7,6},{8,9},{9,8},{10,11... | collective-permute-start | bytes 983048 | tf_op jit(solution)/shard_map/ppermute | solution.py:24
  9.7 16.3 %collective-permute-start.5 = (bf16[40,4096]{1,0:T(8,128)(2,1)}, bf16[40,4096]{1,0:T(8,128)(2,1)S(1)}, u32[]{:S(2)}, u32[]{:S(2)}) collective-permute-start(bf16[40,4096]{1,0:T(8,128)(2,1)} %param.20), channel_id=1, source_target_pairs={{0,1},{1,0},{2,3},{3,2},{4,5},{5,4},{6,7},{7,6},{8,9},{9,8},{10,11... | collective-permute-start | bytes 983048 | tf_op jit(solution)/shard_map/ppermute | solution.py:24
  19.7 15.7 %collective-permute-start.1 = (bf16[80,4096]{1,0:T(8,128)(2,1)}, bf16[80,4096]{1,0:T(8,128)(2,1)S(1)}, u32[]{:S(2)}, u32[]{:S(2)}) collective-permute-start(bf16[80,4096]{1,0:T(8,128)(2,1)} %get-tuple-element.101), channel_id=1, source_target_pairs={{0,8},{1,9},{2,10},{3,11},{4,12},{5,13},{6,14},{7,15},{8,16},{9,17... | collective-permute-start | bytes 1966088 | tf_op jit(solution)/shard_map/ppermute | solution.py:24
  21.3 15.0 %collective-permute-start.2 = (bf16[80,4096]{1,0:T(8,128)(2,1)}, bf16[80,4096]{1,0:T(8,128)(2,1)}, u32[]{:S(2)}, u32[]{:S(2)}) collective-permute-start(bf16[80,4096]{1,0:T(8,128)(2,1)} %get-tuple-element.101), channel_id=1, source_target_pairs={{0,24},{1,25},{2,26},{3,27},{4,28},{5,29},{6,30},{7,31},{8,0},{9,1... | collective-permute-start | bytes 1966088 | tf_op jit(solution)/shard_map/ppermute | solution.py:24
  26.8 17.0 %collective-permute-start.6 = (bf16[80,4096]{1,0:T(8,128)(2,1)}, bf16[80,4096]{1,0:T(8,128)(2,1)}, u32[]{:S(2)}, u32[]{:S(2)}) collective-permute-start(bf16[80,4096]{1,0:T(8,128)(2,1)} %get-tuple-element.98), channel_id=1, source_target_pairs={{0,2},{1,3},{2,4},{3,5},{4,6},{5,7},{6,0},{7,1},{8,10},{9,11},{10,... | collective-permute-start | bytes 1966088 | tf_op jit(solution)/shard_map/ppermute | solution.py:24
  28.9 15.9 %collective-permute-start.8 = (bf16[80,4096]{1,0:T(8,128)(2,1)}, bf16[80,4096]{1,0:T(8,128)(2,1)}, u32[]{:S(2)}, u32[]{:S(2)}) collective-permute-start(bf16[80,4096]{1,0:T(8,128)(2,1)} %get-tuple-element.98), channel_id=1, source_target_pairs={{0,6},{1,7},{2,0},{3,1},{4,2},{5,3},{6,4},{7,5},{8,14},{9,15},{10,... | collective-permute-start | bytes 1966088 | tf_op jit(solution)/shard_map/ppermute | solution.py:24
  35.5 18.8 %collective-permute-start.3 = (bf16[40,4096]{1,0:T(8,128)(2,1)S(1)}, bf16[40,4096]{1,0:T(8,128)(2,1)S(1)}, u32[]{:S(2)}, u32[]{:S(2)}) collective-permute-start(bf16[40,4096]{1,0:T(8,128)(2,1)S(1)} %slice.248), channel_id=1, source_target_pairs={{0,8},{1,9},{2,10},{3,11},{4,12},{5,13},{6,14},{7,15},{8,16},{9,17... | collective-permute-start | bytes 983048 | tf_op jit(solution)/shard_map/ppermute | solution.py:24
  37.3 17.9 %collective-permute-start.4 = (bf16[40,4096]{1,0:T(8,128)(2,1)S(1)}, bf16[40,4096]{1,0:T(8,128)(2,1)S(1)}, u32[]{:S(2)}, u32[]{:S(2)}) collective-permute-start(bf16[40,4096]{1,0:T(8,128)(2,1)S(1)} %slice.249), channel_id=1, source_target_pairs={{0,24},{1,25},{2,26},{3,27},{4,28},{5,29},{6,30},{7,31},{8,0},{9,1... | collective-permute-start | bytes 983048 | tf_op jit(solution)/shard_map/ppermute | solution.py:24
  44.8 11.3 %collective-permute-start.7 = (bf16[40,4096]{1,0:T(8,128)(2,1)S(1)}, bf16[40,4096]{1,0:T(8,128)(2,1)S(1)}, u32[]{:S(2)}, u32[]{:S(2)}) collective-permute-start(bf16[40,4096]{1,0:T(8,128)(2,1)S(1)} %slice.250), channel_id=1, source_target_pairs={{0,2},{1,3},{2,4},{3,5},{4,6},{5,7},{6,0},{7,1},{8,10},{9,11},{10,... | collective-permute-start | bytes 983048 | tf_op jit(solution)/shard_map/ppermute | solution.py:24
  45.9 10.2 %collective-permute-start.9 = (bf16[40,4096]{1,0:T(8,128)(2,1)S(1)}, bf16[40,4096]{1,0:T(8,128)(2,1)S(1)}, u32[]{:S(2)}, u32[]{:S(2)}) collective-permute-start(bf16[40,4096]{1,0:T(8,128)(2,1)S(1)} %slice.252), channel_id=1, source_target_pairs={{0,6},{1,7},{2,0},{3,1},{4,2},{5,3},{6,4},{7,5},{8,14},{9,15},{10,... | collective-permute-start | bytes 983048 | tf_op jit(solution)/shard_map/ppermute | solution.py:24
  57.4 55.8 %collective-permute-start.10 = (bf16[320,4096]{1,0:T(8,128)(2,1)}, bf16[320,4096]{1,0:T(8,128)(2,1)S(1)}, u32[]{:S(2)}, u32[]{:S(2)}) collective-permute-start(bf16[320,4096]{1,0:T(8,128)(2,1)} %fusion.24.refs_0_), channel_id=1, source_target_pairs={{0,2},{1,3},{2,4},{3,5},{4,6},{5,7},{6,0},{7,1},{8,10},{9,11},{10,... | collective-permute-start | bytes 7864328 | tf_op jit(solution)/shard_map/ppermute | solution.py:24
  57.4 57.1 %collective-permute-start.11 = (bf16[320,4096]{1,0:T(8,128)(2,1)}, bf16[320,4096]{1,0:T(8,128)(2,1)}, u32[]{:S(2)}, u32[]{:S(2)}) collective-permute-start(bf16[320,4096]{1,0:T(8,128)(2,1)} %fusion.24.refs_0_), channel_id=1, source_target_pairs={{0,6},{1,7},{2,0},{3,1},{4,2},{5,3},{6,4},{7,5},{8,14},{9,15},{10,... | collective-permute-start | bytes 7864328 | tf_op jit(solution)/shard_map/ppermute | solution.py:24
  63.4 56.9 %collective-permute-start.14 = (bf16[320,4096]{1,0:T(8,128)(2,1)}, bf16[320,4096]{1,0:T(8,128)(2,1)}, u32[]{:S(2)}, u32[]{:S(2)}) collective-permute-start(bf16[320,4096]{1,0:T(8,128)(2,1)} %fusion.25.refs_4_), channel_id=1, source_target_pairs={{0,8},{1,9},{2,10},{3,11},{4,12},{5,13},{6,14},{7,15},{8,16},{9,17... | collective-permute-start | bytes 7864328 | tf_op jit(solution)/shard_map/ppermute | solution.py:24
  64.9 59.4 %collective-permute-start.15 = (bf16[320,4096]{1,0:T(8,128)(2,1)}, bf16[320,4096]{1,0:T(8,128)(2,1)}, u32[]{:S(2)}, u32[]{:S(2)}) collective-permute-start(bf16[320,4096]{1,0:T(8,128)(2,1)} %fusion.25.refs_4_), channel_id=1, source_target_pairs={{0,24},{1,25},{2,26},{3,27},{4,28},{5,29},{6,30},{7,31},{8,0},{9,1... | collective-permute-start | bytes 7864328 | tf_op jit(solution)/shard_map/ppermute | solution.py:24
  113.2 55.1 %copy-start.4 = (bf16[320,4096]{1,0:T(8,128)(2,1)}, bf16[320,4096]{1,0:T(8,128)(2,1)S(1)}, u32[]{:S(2)}) copy-start(bf16[320,4096]{1,0:T(8,128)(2,1)S(1)} %collective-permute-done.10.refs_1_) | copy-start | bytes 7864324
  114.5 42.5 %collective-permute-start.12 = (bf16[160,4096]{1,0:T(8,128)(2,1)}, bf16[160,4096]{1,0:T(8,128)(2,1)}, u32[]{:S(2)}, u32[]{:S(2)}) collective-permute-start(bf16[160,4096]{1,0:T(8,128)(2,1)} %slice.254), channel_id=1, source_target_pairs={{0,2},{1,3},{2,4},{3,5},{4,6},{5,7},{6,0},{7,1},{8,10},{9,11},{10,... | collective-permute-start | bytes 3932168 | tf_op jit(solution)/shard_map/ppermute | solution.py:24
  117.1 11.5 %copy-start.14 = (bf16[4096,448]{0,1:T(8,128)(2,1)S(1)}, bf16[4096,448]{0,1:T(8,128)(2,1)}, u32[]{:S(2)}) copy-start(bf16[4096,448]{0,1:T(8,128)(2,1)} %param.21) | copy-start | bytes 11010052
  117.1 39.9 %collective-permute-start.13 = (bf16[160,4096]{1,0:T(8,128)(2,1)}, bf16[160,4096]{1,0:T(8,128)(2,1)}, u32[]{:S(2)}, u32[]{:S(2)}) collective-permute-start(bf16[160,4096]{1,0:T(8,128)(2,1)} %slice.255), channel_id=1, source_target_pairs={{0,6},{1,7},{2,0},{3,1},{4,2},{5,3},{6,4},{7,5},{8,14},{9,15},{10,... | collective-permute-start | bytes 3932168 | tf_op jit(solution)/shard_map/ppermute | solution.py:24
  122.8 37.0 %collective-permute-start.18 = (bf16[160,4096]{1,0:T(8,128)(2,1)}, bf16[160,4096]{1,0:T(8,128)(2,1)}, u32[]{:S(2)}, u32[]{:S(2)}) collective-permute-start(bf16[160,4096]{1,0:T(8,128)(2,1)} %slice.268), channel_id=1, source_target_pairs={{0,8},{1,9},{2,10},{3,11},{4,12},{5,13},{6,14},{7,15},{8,16},{9,17... | collective-permute-start | bytes 3932168 | tf_op jit(solution)/shard_map/ppermute | solution.py:24
  126.7 33.1 %collective-permute-start.19 = (bf16[160,4096]{1,0:T(8,128)(2,1)}, bf16[160,4096]{1,0:T(8,128)(2,1)}, u32[]{:S(2)}, u32[]{:S(2)}) collective-permute-start(bf16[160,4096]{1,0:T(8,128)(2,1)} %slice.269), channel_id=1, source_target_pairs={{0,24},{1,25},{2,26},{3,27},{4,28},{5,29},{6,30},{7,31},{8,0},{9,1... | collective-permute-start | bytes 3932168 | tf_op jit(solution)/shard_map/ppermute | solution.py:24
  135.0 4.6 %copy-start.16 = (bf16[4096,448]{0,1:T(8,128)(2,1)S(1)}, bf16[4096,448]{0,1:T(8,128)(2,1)}, u32[]{:S(2)}) copy-start(bf16[4096,448]{0,1:T(8,128)(2,1)} %all-gather.3.cloned.1.call-done) | copy-start | bytes 11010052
  143.8 4.5 %copy-start.18 = (bf16[4096,448]{0,1:T(8,128)(2,1)S(1)}, bf16[4096,448]{0,1:T(8,128)(2,1)}, u32[]{:S(2)}) copy-start(bf16[4096,448]{0,1:T(8,128)(2,1)} %all-gather.5.cloned.1.call-done) | copy-start | bytes 11010052
  148.3 3.4 %copy-start.17 = (bf16[4096,448]{0,1:T(8,128)(2,1)S(1)}, bf16[4096,448]{0,1:T(8,128)(2,1)}, u32[]{:S(2)}) copy-start(bf16[4096,448]{0,1:T(8,128)(2,1)} %all-gather.3.cloned.1.call-done) | copy-start | bytes 11010052
  151.7 3.4 %copy-start.13 = (bf16[320,4096]{1,0:T(8,128)(2,1)S(1)}, bf16[320,4096]{1,0:T(8,128)(2,1)}, u32[]{:S(2)}) copy-start(bf16[320,4096]{1,0:T(8,128)(2,1)} %fusion.25.refs_4_) | copy-start | bytes 7864324
  156.9 2.1 collective-permute-start.16
  159.0 3.9 %copy-start.15 = (bf16[4096,448]{0,1:T(8,128)(2,1)S(1)}, bf16[4096,448]{0,1:T(8,128)(2,1)}, u32[]{:S(2)}) copy-start(bf16[4096,448]{0,1:T(8,128)(2,1)} %param.21) | copy-start | bytes 11010052
  159.0 3.1 %collective-permute-start.17 = (bf16[8,128]{1,0:T(8,128)(2,1)S(1)}, bf16[8,128]{1,0:T(8,128)(2,1)S(1)}, u32[]{:S(2)}, u32[]{:S(2)}) collective-permute-start(bf16[8,128]{1,0:T(8,128)(2,1)S(1)} %collective-permute-done.16), channel_id=1, source_target_pairs={{0,32},{32,0},{64,96},{96,64},{1,33},{33,1},{65,97},{97,65},{2,34}... | collective-permute-start | bytes 6152 | tf_op jit(solution)/shard_map/ppermute | solution.py:32
  177.6 37.6 %collective-permute-start.30 = (f32[2,448,1024]{2,1,0:T(8,128)}, f32[2,448,1024]{2,1,0:T(8,128)}, u32[]{:S(2)}, u32[]{:S(2)}) collective-permute-start(f32[2,448,1024]{2,1,0:T(8,128)} %get-tuple-element.87), channel_id=1, source_target_pairs={{0,32},{32,0},{64,96},{96,64},{1,33},{33,1},{65,97},{97,65},{2,34}... | collective-permute-start | bytes 11010056 | tf_op jit(solution)/shard_map/ppermute | solution.py:32
  177.6 66.1 %collective-permute-start.29 = (f32[2,448,1024]{2,1,0:T(8,128)}, f32[2,448,1024]{2,1,0:T(8,128)}, u32[]{:S(2)}, u32[]{:S(2)}) collective-permute-start(f32[2,448,1024]{2,1,0:T(8,128)} %get-tuple-element.85), channel_id=1, source_target_pairs={{0,32},{32,0},{64,96},{96,64},{1,33},{33,1},{65,97},{97,65},{2,34}... | collective-permute-start | bytes 11010056 | tf_op jit(solution)/shard_map/ppermute | solution.py:32
  179.8 28.6 %copy-start.19 = (s32[4]{0:T(128)S(1)}, s32[4]{0:T(128)}, u32[]{:S(2)}) copy-start(s32[4]{0:T(128)} %param.24) | copy-start | bytes 52
  179.8 70.3 %copy-start.3 = (bf16[2,1024,448]{1,2,0:T(8,128)(2,1)S(1)}, bf16[2,1024,448]{1,2,0:T(8,128)(2,1)}, u32[]{:S(2)}) copy-start(bf16[2,1024,448]{1,2,0:T(8,128)(2,1)} %param.25) | copy-start | bytes 5505028
  190.5 3.8 %collective-permute-start.20 = (f32[8,128]{1,0:T(8,128)S(1)}, f32[8,128]{1,0:T(8,128)S(1)}, u32[]{:S(2)}, u32[]{:S(2)}) collective-permute-start(f32[8,128]{1,0:T(8,128)S(1)} %broadcast_in_dim.6), channel_id=1, source_target_pairs={{0,1},{1,0},{2,3},{3,2},{4,5},{5,4},{6,7},{7,6},{8,9},{9,8},{10,11... | collective-permute-start | bytes 12296 | tf_op jit(solution)/shard_map/ppermute | solution.py:28
  194.9 4.8 %collective-permute-start.21 = (f32[8,128]{1,0:T(8,128)S(1)}, f32[8,128]{1,0:T(8,128)S(1)}, u32[]{:S(2)}, u32[]{:S(2)}) collective-permute-start(f32[8,128]{1,0:T(8,128)S(1)} %broadcast_add_fusion), channel_id=1, source_target_pairs={{0,8},{1,9},{2,10},{3,11},{4,12},{5,13},{6,14},{7,15},{8,0},{9,1},... | collective-permute-start | bytes 12296 | tf_op jit(solution)/shard_map/ppermute | solution.py:28
  195.4 5.1 %collective-permute-start.22 = (f32[8,128]{1,0:T(8,128)S(1)}, f32[8,128]{1,0:T(8,128)S(1)}, u32[]{:S(2)}, u32[]{:S(2)}) collective-permute-start(f32[8,128]{1,0:T(8,128)S(1)} %broadcast_add_fusion), channel_id=1, source_target_pairs={{0,16},{1,17},{2,18},{3,19},{4,20},{5,21},{6,22},{7,23},{8,24},{9,... | collective-permute-start | bytes 12296 | tf_op jit(solution)/shard_map/ppermute | solution.py:28
  198.1 4.8 %collective-permute-start.23 = (f32[8,128]{1,0:T(8,128)S(1)}, f32[8,128]{1,0:T(8,128)S(1)}, u32[]{:S(2)}, u32[]{:S(2)}) collective-permute-start(f32[8,128]{1,0:T(8,128)S(1)} %broadcast_add_fusion), channel_id=1, source_target_pairs={{0,24},{1,25},{2,26},{3,27},{4,28},{5,29},{6,30},{7,31},{8,16},{9,... | collective-permute-start | bytes 12296 | tf_op jit(solution)/shard_map/ppermute | solution.py:28
  203.6 5.4 %collective-permute-start.24 = (f32[8,128]{1,0:T(8,128)S(1)}, f32[8,128]{1,0:T(8,128)S(1)}, u32[]{:S(2)}, u32[]{:S(2)}) collective-permute-start(f32[8,128]{1,0:T(8,128)S(1)} %add_add_fusion.1), channel_id=1, source_target_pairs={{0,2},{1,3},{2,0},{3,1},{4,6},{5,7},{6,4},{7,5},{8,10},{9,11},{10,... | collective-permute-start | bytes 12296 | tf_op jit(solution)/shard_map/ppermute | solution.py:28
  203.7 5.4 %collective-permute-start.25 = (f32[8,128]{1,0:T(8,128)S(1)}, f32[8,128]{1,0:T(8,128)S(1)}, u32[]{:S(2)}, u32[]{:S(2)}) collective-permute-start(f32[8,128]{1,0:T(8,128)S(1)} %add_add_fusion.1), channel_id=1, source_target_pairs={{0,4},{1,5},{2,6},{3,7},{4,0},{5,1},{6,2},{7,3},{8,12},{9,13},{10,... | collective-permute-start | bytes 12296 | tf_op jit(solution)/shard_map/ppermute | solution.py:28
  205.3 4.8 %collective-permute-start.26 = (f32[8,128]{1,0:T(8,128)S(1)}, f32[8,128]{1,0:T(8,128)S(1)}, u32[]{:S(2)}, u32[]{:S(2)}) collective-permute-start(f32[8,128]{1,0:T(8,128)S(1)} %add_add_fusion.1), channel_id=1, source_target_pairs={{0,6},{1,7},{2,4},{3,5},{4,2},{5,3},{6,0},{7,1},{8,14},{9,15},{10,... | collective-permute-start | bytes 12296 | tf_op jit(solution)/shard_map/ppermute | solution.py:28
  210.1 3.2 %collective-permute-start.27 = (f32[8,128]{1,0:T(8,128)S(1)}, f32[8,128]{1,0:T(8,128)S(1)}, u32[]{:S(2)}, u32[]{:S(2)}) collective-permute-start(f32[8,128]{1,0:T(8,128)S(1)} %add_add_fusion), channel_id=1, source_target_pairs={{0,32},{32,0},{64,96},{96,64},{1,33},{33,1},{65,97},{97,65},{2,34}... | collective-permute-start | bytes 12296 | tf_op jit(solution)/shard_map/ppermute | solution.py:32
  215.2 28.5 %copy-start.2 = (f32[2,448,1024]{2,1,0:T(8,128)S(1)}, f32[2,448,1024]{2,1,0:T(8,128)}, u32[]{:S(2)}) copy-start(f32[2,448,1024]{2,1,0:T(8,128)} %get-tuple-element.84.keep) | copy-start | bytes 11010052
  217.9 32.0 %collective-permute-start.31 = (f16[448,1024]{1,0:T(8,128)(2,1)S(1)}, f16[448,1024]{1,0:T(8,128)(2,1)S(1)}, u32[]{:S(2)}, u32[]{:S(2)}) collective-permute-start(f16[448,1024]{1,0:T(8,128)(2,1)S(1)} %fusion.6), channel_id=1, source_target_pairs={{0,64},{32,96},{64,0},{96,32},{1,65},{33,97},{65,1},{97,33},{2,66}... | collective-permute-start | bytes 2752520 | tf_op jit(solution)/shard_map/ppermute | solution.py:36
  221.3 21.1 %collective-permute-start.28 = (f32[8,128]{1,0:T(8,128)S(1)}, f32[8,128]{1,0:T(8,128)S(1)}, u32[]{:S(2)}, u32[]{:S(2)}) collective-permute-start(f32[8,128]{1,0:T(8,128)S(1)} %broadcast_in_dim.7), channel_id=1, source_target_pairs={{0,64},{32,96},{64,0},{96,32},{1,65},{33,97},{65,1},{97,33},{2,66}... | collective-permute-start | bytes 12296 | tf_op jit(solution)/shard_map/ppermute | solution.py:36
  243.7 6.4 %copy-start.1 = (f32[2,1024,448]{1,2,0:T(8,128)S(1)}, f32[2,1024,448]{1,2,0:T(8,128)}, u32[]{:S(2)}) copy-start(f32[2,1024,448]{1,2,0:T(8,128)} %param.27) | copy-start | bytes 11010052
  245.3 4.8 %copy-start = (f32[2,1024,448]{1,2,0:T(8,128)S(1)}, f32[2,1024,448]{1,2,0:T(8,128)}, u32[]{:S(2)}) copy-start(f32[2,1024,448]{1,2,0:T(8,128)} %param.26) | copy-start | bytes 11010052
  245.3 15.2 %collective-permute-start.33 = (f16[256,1024]{1,0:T(8,128)(2,1)S(1)}, f16[256,1024]{1,0:T(8,128)(2,1)S(1)}, u32[]{:S(2)}, u32[]{:S(2)}) collective-permute-start(f16[256,1024]{1,0:T(8,128)(2,1)S(1)} %fusion.10), channel_id=1, source_target_pairs={{0,64},{32,96},{64,0},{96,32},{1,65},{33,97},{65,1},{97,33},{2,66}... | collective-permute-start | bytes 1572872 | tf_op jit(solution)/shard_map/ppermute | solution.py:36
  259.1 12.0 %collective-permute-start.32 = (f16[192,1024]{1,0:T(8,128)(2,1)S(1)}, f16[192,1024]{1,0:T(8,128)(2,1)S(1)}, u32[]{:S(2)}, u32[]{:S(2)}) collective-permute-start(f16[192,1024]{1,0:T(8,128)(2,1)S(1)} %fusion.12), channel_id=1, source_target_pairs={{0,64},{32,96},{64,0},{96,32},{1,65},{33,97},{65,1},{97,33},{2,66}... | collective-permute-start | bytes 1179656 | tf_op jit(solution)/shard_map/ppermute | solution.py:36
  (8 other events, 15.2 us)
Sparse Core Ops, SparseCore 0:
  9.7 38.7 all-gather.2
  50.2 35.3 all-gather.4
where the time goes:
time: 283 us; the launch traced here: 282 us
  waiting for transfers between devices  92.3 us (33%)
  starting transfers between devices  51.1 us (18%)
  matrix products  37.2 us (13%)
  Pallas kernels  33.1 us (12%)
  local copies, waits for them, and re-layouts  32.3 us (11%)
  between operations  17.9 us (6%)
  other arithmetic  17.7 us (6%)
    ppermute x18, waiting for transfers between devices, send(): lax.ppermute(value, 'mp', pairs(lambda x, z, y: (x + dx, z + dz, y + dy)))  57.9 us
    dot_general x12, matrix products, rows_dot(): lax.dot_general(rows, weight, (((1,), (0,)), ((), ())), preferred_element...  37.2 us
    ppermute x18, starting transfers between devices, send(): lax.ppermute(value, 'mp', pairs(lambda x, z, y: (x + dx, z + dz, y + dy)))  30 us
    ppermute x4, waiting for transfers between devices, swap_far(): return lax.ppermute(value, 'client', [(c, c ^ 2) for c in range(4)])  27.9 us
    pallas_call x2, Pallas kernels, deltas(): pl.pallas_call(kernel, grid_spec=pltpu.PrefetchScalarGridSpec(num_scalar_...  18.6 us
    unnamed x49, local copies, waits for them, and re-layouts  15 us
    pallas_call x3, Pallas kernels, adam(): pl.pallas_call(kernel, grid=(units // block,), in_specs=[pl.BlockSpec(mem...  13.7 us
    slice x8, local copies, waits for them, and re-layouts, ring(): return [block, below, above, below[:half], above[half:]]  11.9 us
  transfers between devices with their start and end apart: 36, of which 12 were waited for; matrix products, arithmetic and copies ran while one was open for 28% of the time, Pallas kernels for 7%

commit v1 on v0

--- a/solution.py
+++ b/solution.py
@@ -26,6 +26,12 @@
 
 def flip(value, bx=0, bz=0, by=0):
     return lax.ppermute(value, "mp", pairs(lambda x, z, y: (x ^ bx, z ^ bz, y ^ by)))
+
+
+def both(value, by):
+    to = [((c, m), (c ^ 1, m ^ 1 if by else m)) for c in range(4) for m in range(NX * NZ * NY)]
+    wide = NX * NZ * NY
+    return lax.ppermute(value, ("client", "mp"), [(a[0] * wide + a[1], b[0] * wide + b[1]) for a, b in to])
 
 
 def swap_core(value):
@@ -143,7 +149,7 @@
     def kernel(factors, keep, received, arrived, noise, first, second, *refs):
         new_first, new_second, step = refs[-3:]
         average = noise[0].astype(F32) + (
-            (factors[0] * keep[0] + factors[1] * received[0]) + arrived[...] * factors[2]
+            (factors[:1, :1] * keep[0] + factors[8:9, :1] * received[0]) + arrived[...] * factors[16:17, :1]
         )
         moment = 0.9 * first[0] + 0.1 * average
         spread = 0.99 * second[0] + 0.01 * average * average
@@ -158,7 +164,7 @@
         kernel,
         grid=(units // block,),
         in_specs=[
-            pl.BlockSpec(memory_space=pltpu.SMEM),
+            pl.BlockSpec((24, 128), lambda i: (0, 0)),
             zero,
             zero,
             pl.BlockSpec((block, width), lambda i: (i, 0)),
@@ -211,23 +217,24 @@
     up_received, down_received = swap_core(up_sent), swap_core(down_sent)
     up_kept, down_kept, more = deltas(xs, ys, up_input, hidden, here + core, width)
 
-    client_total = jnp.full((8, 128), jnp.sum(squares + more), F32)
-    client_total = client_total + flip(client_total, by=1)
+    partial = jnp.full((8, 128), jnp.sum(squares + more), F32)
+    beside = flip(partial, by=1)
+    across, aside = both(partial, False), both(partial, True)
+    totals = jnp.concatenate([partial + beside, across + aside], axis=0)
     for axis in ("bx", "bz"):
-        others = [flip(client_total, **{axis: b}) for b in (1, 2, 3)]
-        client_total = (client_total + others[0]) + (others[1] + others[2])
-    other_total = swap_core(client_total)
+        others = [flip(totals, **{axis: b}) for b in (1, 2, 3)]
+        totals = (totals + others[0]) + (others[1] + others[2])
     clip_bound = math.sqrt(2.0 * model_width * hidden_units * token_count)
     weights = counts.astype(F32)
     shares = weights / jnp.sum(weights)
-    norm_own, norm_other = jnp.sqrt(client_total[0, 0]), jnp.sqrt(other_total[0, 0])
-    w_own = shares[member] * (clip_bound / jnp.maximum(norm_own, clip_bound))
-    w_other = shares[member ^ 1] * (clip_bound / jnp.maximum(norm_other, clip_bound))
-    most = w_own * norm_own + w_other * norm_other
+    share = jnp.repeat(jnp.stack([shares[member], shares[member ^ 1]]), 8)[:, None]
+    norms = jnp.sqrt(totals)
+    factor = share * (clip_bound / jnp.maximum(norms, clip_bound))
+    most = factor[:8] * norms[:8] + factor[8:] * norms[8:]
     power = 14.0 - jnp.ceil(jnp.log2(jnp.where(most > 0.0, most, 1.0)))
     scale = jnp.exp2(jnp.clip(power, -100.0, 100.0))
-    their_scale = swap_far(jnp.full((8, 128), scale, F32))[0, 0]
-    factors = jnp.stack([w_own, w_other, 1.0 / their_scale])
+    factors = jnp.concatenate([factor, 1.0 / swap_far(scale)], axis=0)
+    w_own, w_other, scale = factor[:1, :1], factor[8:9, :1], scale[:1, :1]
 
     def weighted(kept, received, rows):
         total = (w_own * kept[1, rows] + w_other * received[1, rows]) * scale
@@ -236,10 +243,12 @@
     cut = 256
     turn = lambda a: a.transpose(0, 2, 1)
     states = [turn(a) for a in (noise, first_moment, second_moment)]
-    up_arrived = swap_far(weighted(up_kept, up_received, slice(None))).astype(F32)
-    down_low = swap_far(weighted(down_kept, down_received, slice(0, cut))).astype(F32)
+    up_arrived = swap_far(weighted(up_kept, up_received, slice(None)))
+    down = [weighted(down_kept, down_received, rows) for rows in (slice(0, cut), slice(cut, None))]
+    down_low, down_high = lax.optimization_barrier(down)
+    up_arrived = held(up_arrived, token(down_low, down_high)).astype(F32)
+    down_low = swap_far(down_low).astype(F32)
     outs = adam(0, 0, factors, up_kept, up_received, up_arrived, *states, None)
-    down_high = weighted(down_kept, down_received, slice(cut, None))
     down_high = swap_far(held(down_high, jnp.minimum(jnp.abs(outs[0][0, :8, :128]), 0.0))).astype(F32)
     outs = adam(1, 0, factors, down_kept, down_received, down_low, *states, outs)
     outs = adam(1, cut, factors, down_kept, down_received, down_high, *states, outs)

time: 283 us -> 275 us (0.972)
  waiting for transfers between devices: 92.3 us -> 81.2 us
  other arithmetic: 17.7 us -> 24 us
  between operations: 17.9 us -> 14.5 us
    ppermute x4, waiting for transfers between devices: 27.9 us -> 17.1 us  [swap_far(): return lax.ppermute(value, 'client', [(c, c ^ 2) for c in range(4)])]
    convert_element_type x3, other arithmetic: 5.57 us -> 11.4 us  [weighted(): return total.astype(jnp.float16)]
    ppermute x7, waiting for transfers between devices: 5.84 us -> 2.29 us  [flip(): lax.ppermute(value, 'mp', pairs(lambda x, z, y: (x ^ bx, z ^ bz, y ^ by)))]
  transfers between devices with their start and end apart: 36 -> 39, of which waited for: 12 -> 12; matrix products, arithmetic and copies ran while one was open for 28% -> 31% of each run, Pallas kernels for 7% -> 7%
where the time goes in v1:
time: 275 us; the launch traced here: 273 us
  waiting for transfers between devices  81.2 us (30%)
  starting transfers between devices  51 us (19%)
  matrix products  37.2 us (14%)
  Pallas kernels  33.4 us (12%)
  local copies, waits for them, and re-layouts  31.9 us (12%)
  other arithmetic  24 us (9%)
  between operations  14.5 us (5%)
    ppermute x18, waiting for transfers between devices, send(): lax.ppermute(value, 'mp', pairs(lambda x, z, y: (x + dx, z + dz, y + dy)))  57.9 us
    dot_general x12, matrix products, rows_dot(): lax.dot_general(rows, weight, (((1,), (0,)), ((), ())), preferred_element...  37.2 us
    ppermute x18, starting transfers between devices, send(): lax.ppermute(value, 'mp', pairs(lambda x, z, y: (x + dx, z + dz, y + dy)))  30 us
    pallas_call x2, Pallas kernels, deltas(): pl.pallas_call(kernel, grid_spec=pltpu.PrefetchScalarGridSpec(num_scalar_...  18.6 us
    ppermute x4, waiting for transfers between devices, swap_far(): return lax.ppermute(value, 'client', [(c, c ^ 2) for c in range(4)])  17.1 us
    unnamed x49, local copies, waits for them, and re-layouts  15 us
    pallas_call x3, Pallas kernels, adam(): pl.pallas_call(kernel, grid=(units // block,), in_specs=[pl.BlockSpec((24...  14 us
    slice x8, local copies, waits for them, and re-layouts, ring(): return [block, below, above, below[:half], above[half:]]  11.9 us
  transfers between devices with their start and end apart: 39, of which 12 were waited for; matrix products, arithmetic and copies ran while one was open for 31% of the time, Pallas kernels for 7%

profile of v1, /device:TPU:0, one launch (start us, length us, event | category | flops | bytes accessed | tf_op | source)
XLA Modules:
  0.0 273.2 jit_solution(4442823630666797649)
XLA Ops:
  7.9 1.7 collective-permute-start
  10.0 1.9 constant_dynamic-update-slice_fusion.1
  11.9 1.7 constant_dynamic-update-slice_fusion.15
  13.7 5.2 %collective-permute-done = bf16[40,4096]{1,0:T(8,128)(2,1)S(1)} collective-permute-done((bf16[40,4096]{1,0:T(8,128)(2,1)}, bf16[40,4096]{1,0:T(8,128)(2,1)S(1)}, u32[]{:S(2)}, u32[]{:S(2)}) %collective-permute-start) | collective-permute-done | bytes 327712 | tf_op jit(solution)/shard_map/ppermute | solution.py:24
  23.0 3.0 %collective-permute-done.5 = bf16[40,4096]{1,0:T(8,128)(2,1)S(1)} collective-permute-done((bf16[40,4096]{1,0:T(8,128)(2,1)}, bf16[40,4096]{1,0:T(8,128)(2,1)S(1)}, u32[]{:S(2)}, u32[]{:S(2)}) %collective-permute-start.5) | collective-permute-done | bytes 327712 | tf_op jit(solution)/shard_map/ppermute | solution.py:24
  26.8 2.1 collective-permute-start.6
  28.9 2.9 %collective-permute-start.8 = (bf16[80,4096]{1,0:T(8,128)(2,1)}, bf16[80,4096]{1,0:T(8,128)(2,1)}, u32[]{:S(2)}, u32[]{:S(2)}) collective-permute-start(bf16[80,4096]{1,0:T(8,128)(2,1)} %get-tuple-element.116), channel_id=1, source_target_pairs={{0,6},{1,7},{2,0},{3,1},{4,2},{5,3},{6,4},{7,5},{8,14},{9,15},{10,... | collective-permute-start | bytes 1966088 | tf_op jit(solution)/shard_map/ppermute | solution.py:24
  31.8 3.7 %collective-permute-done.1 = bf16[80,4096]{1,0:T(8,128)(2,1)S(1)} collective-permute-done((bf16[80,4096]{1,0:T(8,128)(2,1)}, bf16[80,4096]{1,0:T(8,128)(2,1)S(1)}, u32[]{:S(2)}, u32[]{:S(2)}) %collective-permute-start.1) | collective-permute-done | bytes 655392 | tf_op jit(solution)/shard_map/ppermute | solution.py:24
  37.3 2.6 collective-permute-start.4
  39.9 3.9 %collective-permute-done.6 = bf16[80,4096]{1,0:T(8,128)(2,1)} collective-permute-done((bf16[80,4096]{1,0:T(8,128)(2,1)}, bf16[80,4096]{1,0:T(8,128)(2,1)}, u32[]{:S(2)}, u32[]{:S(2)}) %collective-permute-start.6) | collective-permute-done | bytes 655392 | tf_op jit(solution)/shard_map/ppermute | solution.py:24
  45.9 3.3 %collective-permute-start.9 = (bf16[40,4096]{1,0:T(8,128)(2,1)S(1)}, bf16[40,4096]{1,0:T(8,128)(2,1)S(1)}, u32[]{:S(2)}, u32[]{:S(2)}) collective-permute-start(bf16[40,4096]{1,0:T(8,128)(2,1)S(1)} %slice.300), channel_id=1, source_target_pairs={{0,6},{1,7},{2,0},{3,1},{4,2},{5,3},{6,4},{7,5},{8,14},{9,15},{10,... | collective-permute-start | bytes 983048 | tf_op jit(solution)/shard_map/ppermute | solution.py:24
  50.0 2.0 constant_dynamic-update-slice_fusion.4
  57.3 3.2 %collective-permute-start.11 = (bf16[320,4096]{1,0:T(8,128)(2,1)}, bf16[320,4096]{1,0:T(8,128)(2,1)}, u32[]{:S(2)}, u32[]{:S(2)}) collective-permute-start(bf16[320,4096]{1,0:T(8,128)(2,1)} %fusion.32.refs_0_), channel_id=1, source_target_pairs={{0,6},{1,7},{2,0},{3,1},{4,2},{5,3},{6,4},{7,5},{8,14},{9,15},{10,... | collective-permute-start | bytes 7864328 | tf_op jit(solution)/shard_map/ppermute | solution.py:24
  64.8 1.7 collective-permute-start.15
  66.7 4.4 %fusion.38.refs_0_ = f32[320,448]{1,0:T(8,128)S(1)} fusion(bf16[320,4096]{1,0:T(8,128)(2,1)} %fusion.32.refs_0_, bf16[4096,448]{0,1:T(8,128)(2,1)} %param.23), kind=kOutput, calls=%fused_computation.96 | convolution fusion | flops 1174405120 | bytes 6864896 | tf_op jit(solution)/shard_map/dot_general | solution.py:77
  71.1 42.1 %collective-permute-done.10.refs_1_ = bf16[320,4096]{1,0:T(8,128)(2,1)S(1)} collective-permute-done((bf16[320,4096]{1,0:T(8,128)(2,1)}, bf16[320,4096]{1,0:T(8,128)(2,1)S(1)}, u32[]{:S(2)}, u32[]{:S(2)}) %collective-permute-start.10) | collective-permute-done | bytes 2621472 | tf_op jit(solution)/shard_map/ppermute | solution.py:24
  114.4 2.6 slice.303
  117.0 3.2 %collective-permute-start.13 = (bf16[160,4096]{1,0:T(8,128)(2,1)}, bf16[160,4096]{1,0:T(8,128)(2,1)}, u32[]{:S(2)}, u32[]{:S(2)}) collective-permute-start(bf16[160,4096]{1,0:T(8,128)(2,1)} %slice.303), channel_id=1, source_target_pairs={{0,6},{1,7},{2,0},{3,1},{4,2},{5,3},{6,4},{7,5},{8,14},{9,15},{10,... | collective-permute-start | bytes 3932168 | tf_op jit(solution)/shard_map/ppermute | solution.py:24
  120.2 2.5 slice.316
  124.2 2.5 slice.317
  126.7 1.8 collective-permute-start.19
  128.5 2.4 fusion.39.refs_3_
  130.9 4.1 %fusion.40.refs_6_ = f32[320,448]{1,0:T(8,128)} fusion(bf16[320,4096]{1,0:T(8,128)(2,1)} %collective-permute-done.11.refs_2_, bf16[4096,448]{0,1:T(8,128)(2,1)S(1)} %copy-done.14), kind=kOutput, calls=%fused_computation.98 | convolution fusion | flops 1174405120 | bytes 6864896 | tf_op jit(solution)/shard_map/dot_general | solution.py:77
  135.0 4.6 %fusion.42.refs_4_ = f32[320,448]{1,0:T(8,128)} fusion(bf16[320,4096]{1,0:T(8,128)(2,1)S(1)} %collective-permute-done.10.refs_1_, bf16[4096,448]{0,1:T(8,128)(2,1)} %all-gather.3.cloned.1.call-done), kind=kOutput, calls=%fused_computation.100 | convolution fusion | flops 1174405120 | bytes 6864896 | tf_op jit(solution)/shard_map/dot_general | solution.py:77
  139.6 4.2 %fusion.43.refs_7_ = f32[320,448]{1,0:T(8,128)} fusion(bf16[320,4096]{1,0:T(8,128)(2,1)} %collective-permute-done.11.refs_2_, bf16[4096,448]{0,1:T(8,128)(2,1)S(1)} %copy-done.16), kind=kOutput, calls=%fused_computation.101 | convolution fusion | flops 1174405120 | bytes 6864896 | tf_op jit(solution)/shard_map/dot_general | solution.py:77
  143.7 4.5 %fusion.45.refs_5_ = f32[320,448]{1,0:T(8,128)S(1)} fusion(bf16[320,4096]{1,0:T(8,128)(2,1)} %collective-permute-done.14.refs_5_, bf16[4096,448]{0,1:T(8,128)(2,1)} %all-gather.5.cloned.1.call-done), kind=kOutput, calls=%fused_computation.103 | convolution fusion | flops 1174405120 | bytes 6864896 | tf_op jit(solution)/shard_map/dot_general | solution.py:77
  148.3 3.4 %fusion.46.refs_8_ = f32[320,448]{1,0:T(8,128)S(1)} fusion(bf16[320,4096]{1,0:T(8,128)(2,1)} %collective-permute-done.15.refs_6_, bf16[4096,448]{0,1:T(8,128)(2,1)S(1)} %copy-done.18), kind=kOutput, calls=%fused_computation.104 | convolution fusion | flops 1174405120 | bytes 6864896 | tf_op jit(solution)/shard_map/dot_general | solution.py:77
  151.7 3.4 %fusion.41.refs_1_ = f32[320,448]{1,0:T(8,128)S(1)} fusion(bf16[320,4096]{1,0:T(8,128)(2,1)} %fusion.32.refs_0_, bf16[4096,448]{0,1:T(8,128)(2,1)S(1)} %copy-done.17), kind=kOutput, calls=%fused_computation.99 | convolution fusion | flops 1174405120 | bytes 6864896 | tf_op jit(solution)/shard_map/dot_general | solution.py:77
  157.0 2.0 pad_maximum_fusion
  159.8 2.3 pad_maximum_fusion.1
  168.2 9.3 %shard_map.113 = (f32[2,448,1024]{2,1,0:T(8,128)}, f32[2,448,1024]{2,1,0:T(8,128)}, f32[8,128]{1,0:T(8,128)S(1)}) custom-call(s32[2]{0:T(128)S(1)} %get-tuple-element.130._, bf16[320,4096]{1,0:T(8,128)(2,1)} %fusion.32.refs_0_, bf16[320,4096]{1,0:T(8,128)(2,1)S(1)} %collective-permute-done.10.refs_1_, bf16[320,4096]{1,0:T(8,128)(2,1)} %collective-permute-done.11.refs_2_, ...), custom_call_target="tpu_custom_call" | custom-call | flops 4697620480 | bytes 17825792 | tf_op jit(solution)/shard_map/pallas_call | solution.py:127
  179.8 9.3 %shard_map.114 = (f32[2,448,1024]{2,1,0:T(8,128)}, f32[2,448,1024]{2,1,0:T(8,128)}, f32[8,128]{1,0:T(8,128)S(1)}) custom-call(s32[2]{0:T(128)S(1)} %get-tuple-element.129._, bf16[320,4096]{1,0:T(8,128)(2,1)} %fusion.32.refs_0_, bf16[320,4096]{1,0:T(8,128)(2,1)S(1)} %copy-done.5, bf16[320,4096]{1,0:T(8,128)(2,1)} %collective-permute-done.11.refs_2_, ...), custom_call_target="tpu_custom_call" | custom-call | flops 4697620480 | bytes 17825792 | tf_op jit(solution)/shard_map/pallas_call | solution.py:127
  190.3 2.2 collective-permute-start.20
  193.7 1.9 collective-permute-done.22
  196.7 2.7 collective-permute-start.24
  202.2 2.0 collective-permute-done.25
  205.8 3.1 %collective-permute-start.28 = (f32[16,128]{1,0:T(8,128)S(1)}, f32[16,128]{1,0:T(8,128)S(1)}, u32[]{:S(2)}, u32[]{:S(2)}) collective-permute-start(f32[16,128]{1,0:T(8,128)S(1)} %add_add_fusion), channel_id=1, source_target_pairs={{0,6},{1,7},{2,4},{3,5},{4,2},{5,3},{6,0},{7,1},{8,14},{9,15},{10,... | collective-permute-start | bytes 24584 | tf_op jit(solution)/shard_map/ppermute | solution.py:28
  211.3 3.0 %collective-permute-start.29 = (f32[8,128]{1,0:T(8,128)S(1)}, f32[8,128]{1,0:T(8,128)S(1)}, u32[]{:S(2)}, u32[]{:S(2)}) collective-permute-start(f32[8,128]{1,0:T(8,128)S(1)} %fusion.18), channel_id=1, source_target_pairs={{0,64},{32,96},{64,0},{96,32},{1,65},{33,97},{65,1},{97,33},{2,66}... | collective-permute-start | bytes 12296 | tf_op jit(solution)/shard_map/ppermute | solution.py:42
  214.9 4.4 %fusion.6 = f16[448,1024]{1,0:T(8,128)(2,1)S(1)} fusion(f32[2,448,1024]{2,1,0:T(8,128)} %collective-permute-done.31.received, f32[2,448,1024]{2,1,0:T(8,128)} %get-tuple-element.101.keep, f32[]{:T(128)} %bitcast.4, f32[]{:T(128)} %bitcast.3, f32[]{:T(128)} %bitcast.2), kind=kLoop, calls=%fused_computation.10 | loop fusion | flops 2293760 | bytes 4587532 | tf_op jit(solution)/shard_map/convert_element_type | solution.py:241
  219.9 3.4 %fusion.11 = f16[192,1024]{1,0:T(8,128)(2,1)S(1)} fusion(f32[2,448,1024]{2,1,0:T(8,128)} %collective-permute-done.30.received, f32[2,448,1024]{2,1,0:T(8,128)S(1)} %copy-done.2, f32[]{:T(128)} %bitcast.4, f32[]{:T(128)} %bitcast.3, f32[]{:T(128)} %bitcast.2), kind=kLoop, calls=%fused_computation.16 | loop fusion | flops 983040 | bytes 1966092 | tf_op jit(solution)/shard_map/convert_element_type | solution.py:241
  223.3 3.6 %fusion.10 = f16[256,1024]{1,0:T(8,128)(2,1)S(1)} fusion(f32[2,448,1024]{2,1,0:T(8,128)} %collective-permute-done.30.received, f32[2,448,1024]{2,1,0:T(8,128)S(1)} %copy-done.2, f32[]{:T(128)} %bitcast.4, f32[]{:T(128)} %bitcast.3, f32[]{:T(128)} %bitcast.2), kind=kLoop, calls=%fused_computation.15 | loop fusion | flops 1310720 | bytes 2621452 | tf_op jit(solution)/shard_map/convert_element_type | solution.py:241
  228.7 3.0 %collective-permute-start.36 = (f16[256,1024]{1,0:T(8,128)(2,1)S(1)}, f16[256,1024]{1,0:T(8,128)(2,1)S(1)}, u32[]{:S(2)}, u32[]{:S(2)}) collective-permute-start(f16[256,1024]{1,0:T(8,128)(2,1)S(1)} %fusion.10), channel_id=1, source_target_pairs={{0,64},{32,96},{64,0},{96,32},{1,65},{33,97},{65,1},{97,33},{2,66}... | collective-permute-start | bytes 1572872 | tf_op jit(solution)/shard_map/ppermute | solution.py:42
  231.7 12.5 %collective-permute-done.32 = f16[448,1024]{1,0:T(8,128)(2,1)S(1)} collective-permute-done((f16[448,1024]{1,0:T(8,128)(2,1)S(1)}, f16[448,1024]{1,0:T(8,128)(2,1)S(1)}, u32[]{:S(2)}, u32[]{:S(2)}) %collective-permute-start.32) | collective-permute-done | bytes 917536 | tf_op jit(solution)/shard_map/ppermute | solution.py:42
  244.4 2.0 copy-done.6
  246.4 6.4 %shard_map.115 = (f32[2,448,1024]{2,1,0:T(8,128)}, f32[2,448,1024]{2,1,0:T(8,128)}, f32[2,448,1024]{2,1,0:T(8,128)}) custom-call(f32[24,128]{1,0:T(8,128)S(1)} %pad_maximum_fusion.2.factors, f32[2,448,1024]{2,1,0:T(8,128)S(1)} %copy-done.6, f32[2,448,1024]{2,1,0:T(8,128)} %collective-permute-done.31.received, f32[448,1024]{1,0:T(8,128)S(1)} %convert_element_type.67.arrived, ...), custom_call_target="tpu_custom_call" | custom-call | flops 5505024 | bytes 15597568 | tf_op jit(solution)/shard_map/pallas_call | solution.py:163
  254.2 4.1 %shard_map.116 = (f32[2,448,1024]{2,1,0:T(8,128)}, f32[2,448,1024]{2,1,0:T(8,128)}, f32[2,448,1024]{2,1,0:T(8,128)}) custom-call(f32[24,128]{1,0:T(8,128)S(1)} %pad_maximum_fusion.2.factors, f32[2,448,1024]{2,1,0:T(8,128)S(1)} %copy-done.2, ...), custom_call_target="tpu_custom_call", output_to_operand_aliasing={{0}: (7, {}), {1}: (8, {}), {2}: (9, {})} | custom-call | flops 3145728 | bytes 8912896 | tf_op jit(solution)/shard_map/pallas_call | solution.py:163
  258.3 4.6 %collective-permute-done.35 = f16[192,1024]{1,0:T(8,128)(2,1)S(1)} collective-permute-done((f16[192,1024]{1,0:T(8,128)(2,1)S(1)}, f16[192,1024]{1,0:T(8,128)(2,1)S(1)}, u32[]{:S(2)}, u32[]{:S(2)}) %collective-permute-start.35) | collective-permute-done | bytes 393248 | tf_op jit(solution)/shard_map/ppermute | solution.py:42
  262.9 3.5 %shard_map.117 = (f32[2,448,1024]{2,1,0:T(8,128)}, f32[2,448,1024]{2,1,0:T(8,128)}, f32[2,448,1024]{2,1,0:T(8,128)}) custom-call(f32[24,128]{1,0:T(8,128)S(1)} %pad_maximum_fusion.2.factors, f32[2,448,1024]{2,1,0:T(8,128)S(1)} %copy-done.2, ...), custom_call_target="tpu_custom_call", output_to_operand_aliasing={{0}: (7, {}), {1}: (8, {}), {2}: (9, {})} | custom-call | flops 2359296 | bytes 6684672 | tf_op jit(solution)/shard_map/pallas_call | solution.py:163
  (148 shorter events, 49.0 us)
Async XLA Ops:
  7.2 127.8 %all-gather.3.cloned.1.call-start = ((), (), s32[]{:S(2)}) async-start(), calls=%async_computation | async-start | bytes 4587520 | tf_op jit(solution)/shard_map/all_gather | solution.py:193
  7.9 135.8 %all-gather.5.cloned.1.call-start = ((), (), s32[]{:S(2)}) async-start(), calls=%async_computation.1 | async-start | bytes 4587520 | tf_op jit(solution)/shard_map/all_gather | solution.py:194
  7.9 10.9 %collective-permute-start = (bf16[40,4096]{1,0:T(8,128)(2,1)}, bf16[40,4096]{1,0:T(8,128)(2,1)S(1)}, u32[]{:S(2)}, u32[]{:S(2)}) collective-permute-start(bf16[40,4096]{1,0:T(8,128)(2,1)} %param.21), channel_id=1, source_target_pairs={{0,1},{1,0},{2,3},{3,2},{4,5},{5,4},{6,7},{7,6},{8,9},{9,8},{10,11... | collective-permute-start | bytes 983048 | tf_op jit(solution)/shard_map/ppermute | solution.py:24
  9.7 16.3 %collective-permute-start.5 = (bf16[40,4096]{1,0:T(8,128)(2,1)}, bf16[40,4096]{1,0:T(8,128)(2,1)S(1)}, u32[]{:S(2)}, u32[]{:S(2)}) collective-permute-start(bf16[40,4096]{1,0:T(8,128)(2,1)} %param.22), channel_id=1, source_target_pairs={{0,1},{1,0},{2,3},{3,2},{4,5},{5,4},{6,7},{7,6},{8,9},{9,8},{10,11... | collective-permute-start | bytes 983048 | tf_op jit(solution)/shard_map/ppermute | solution.py:24
  19.7 15.7 %collective-permute-start.1 = (bf16[80,4096]{1,0:T(8,128)(2,1)}, bf16[80,4096]{1,0:T(8,128)(2,1)S(1)}, u32[]{:S(2)}, u32[]{:S(2)}) collective-permute-start(bf16[80,4096]{1,0:T(8,128)(2,1)} %get-tuple-element.119), channel_id=1, source_target_pairs={{0,8},{1,9},{2,10},{3,11},{4,12},{5,13},{6,14},{7,15},{8,16},{9,17... | collective-permute-start | bytes 1966088 | tf_op jit(solution)/shard_map/ppermute | solution.py:24
  21.3 15.0 %collective-permute-start.2 = (bf16[80,4096]{1,0:T(8,128)(2,1)}, bf16[80,4096]{1,0:T(8,128)(2,1)}, u32[]{:S(2)}, u32[]{:S(2)}) collective-permute-start(bf16[80,4096]{1,0:T(8,128)(2,1)} %get-tuple-element.119), channel_id=1, source_target_pairs={{0,24},{1,25},{2,26},{3,27},{4,28},{5,29},{6,30},{7,31},{8,0},{9,1... | collective-permute-start | bytes 1966088 | tf_op jit(solution)/shard_map/ppermute | solution.py:24
  26.8 17.0 %collective-permute-start.6 = (bf16[80,4096]{1,0:T(8,128)(2,1)}, bf16[80,4096]{1,0:T(8,128)(2,1)}, u32[]{:S(2)}, u32[]{:S(2)}) collective-permute-start(bf16[80,4096]{1,0:T(8,128)(2,1)} %get-tuple-element.116), channel_id=1, source_target_pairs={{0,2},{1,3},{2,4},{3,5},{4,6},{5,7},{6,0},{7,1},{8,10},{9,11},{10,... | collective-permute-start | bytes 1966088 | tf_op jit(solution)/shard_map/ppermute | solution.py:24
  28.9 15.9 %collective-permute-start.8 = (bf16[80,4096]{1,0:T(8,128)(2,1)}, bf16[80,4096]{1,0:T(8,128)(2,1)}, u32[]{:S(2)}, u32[]{:S(2)}) collective-permute-start(bf16[80,4096]{1,0:T(8,128)(2,1)} %get-tuple-element.116), channel_id=1, source_target_pairs={{0,6},{1,7},{2,0},{3,1},{4,2},{5,3},{6,4},{7,5},{8,14},{9,15},{10,... | collective-permute-start | bytes 1966088 | tf_op jit(solution)/shard_map/ppermute | solution.py:24
  35.5 18.8 %collective-permute-start.3 = (bf16[40,4096]{1,0:T(8,128)(2,1)S(1)}, bf16[40,4096]{1,0:T(8,128)(2,1)S(1)}, u32[]{:S(2)}, u32[]{:S(2)}) collective-permute-start(bf16[40,4096]{1,0:T(8,128)(2,1)S(1)} %slice.296), channel_id=1, source_target_pairs={{0,8},{1,9},{2,10},{3,11},{4,12},{5,13},{6,14},{7,15},{8,16},{9,17... | collective-permute-start | bytes 983048 | tf_op jit(solution)/shard_map/ppermute | solution.py:24
  37.3 17.8 %collective-permute-start.4 = (bf16[40,4096]{1,0:T(8,128)(2,1)S(1)}, bf16[40,4096]{1,0:T(8,128)(2,1)S(1)}, u32[]{:S(2)}, u32[]{:S(2)}) collective-permute-start(bf16[40,4096]{1,0:T(8,128)(2,1)S(1)} %slice.297), channel_id=1, source_target_pairs={{0,24},{1,25},{2,26},{3,27},{4,28},{5,29},{6,30},{7,31},{8,0},{9,1... | collective-permute-start | bytes 983048 | tf_op jit(solution)/shard_map/ppermute | solution.py:24
  44.8 11.3 %collective-permute-start.7 = (bf16[40,4096]{1,0:T(8,128)(2,1)S(1)}, bf16[40,4096]{1,0:T(8,128)(2,1)S(1)}, u32[]{:S(2)}, u32[]{:S(2)}) collective-permute-start(bf16[40,4096]{1,0:T(8,128)(2,1)S(1)} %slice.298), channel_id=1, source_target_pairs={{0,2},{1,3},{2,4},{3,5},{4,6},{5,7},{6,0},{7,1},{8,10},{9,11},{10,... | collective-permute-start | bytes 983048 | tf_op jit(solution)/shard_map/ppermute | solution.py:24
  45.9 10.1 %collective-permute-start.9 = (bf16[40,4096]{1,0:T(8,128)(2,1)S(1)}, bf16[40,4096]{1,0:T(8,128)(2,1)S(1)}, u32[]{:S(2)}, u32[]{:S(2)}) collective-permute-start(bf16[40,4096]{1,0:T(8,128)(2,1)S(1)} %slice.300), channel_id=1, source_target_pairs={{0,6},{1,7},{2,0},{3,1},{4,2},{5,3},{6,4},{7,5},{8,14},{9,15},{10,... | collective-permute-start | bytes 983048 | tf_op jit(solution)/shard_map/ppermute | solution.py:24
  57.3 55.8 %collective-permute-start.10 = (bf16[320,4096]{1,0:T(8,128)(2,1)}, bf16[320,4096]{1,0:T(8,128)(2,1)S(1)}, u32[]{:S(2)}, u32[]{:S(2)}) collective-permute-start(bf16[320,4096]{1,0:T(8,128)(2,1)} %fusion.32.refs_0_), channel_id=1, source_target_pairs={{0,2},{1,3},{2,4},{3,5},{4,6},{5,7},{6,0},{7,1},{8,10},{9,11},{10,... | collective-permute-start | bytes 7864328 | tf_op jit(solution)/shard_map/ppermute | solution.py:24
  57.3 57.1 %collective-permute-start.11 = (bf16[320,4096]{1,0:T(8,128)(2,1)}, bf16[320,4096]{1,0:T(8,128)(2,1)}, u32[]{:S(2)}, u32[]{:S(2)}) collective-permute-start(bf16[320,4096]{1,0:T(8,128)(2,1)} %fusion.32.refs_0_), channel_id=1, source_target_pairs={{0,6},{1,7},{2,0},{3,1},{4,2},{5,3},{6,4},{7,5},{8,14},{9,15},{10,... | collective-permute-start | bytes 7864328 | tf_op jit(solution)/shard_map/ppermute | solution.py:24
  63.4 56.9 %collective-permute-start.14 = (bf16[320,4096]{1,0:T(8,128)(2,1)}, bf16[320,4096]{1,0:T(8,128)(2,1)}, u32[]{:S(2)}, u32[]{:S(2)}) collective-permute-start(bf16[320,4096]{1,0:T(8,128)(2,1)} %fusion.33.refs_4_), channel_id=1, source_target_pairs={{0,8},{1,9},{2,10},{3,11},{4,12},{5,13},{6,14},{7,15},{8,16},{9,17... | collective-permute-start | bytes 7864328 | tf_op jit(solution)/shard_map/ppermute | solution.py:24
  64.8 59.3 %collective-permute-start.15 = (bf16[320,4096]{1,0:T(8,128)(2,1)}, bf16[320,4096]{1,0:T(8,128)(2,1)}, u32[]{:S(2)}, u32[]{:S(2)}) collective-permute-start(bf16[320,4096]{1,0:T(8,128)(2,1)} %fusion.33.refs_4_), channel_id=1, source_target_pairs={{0,24},{1,25},{2,26},{3,27},{4,28},{5,29},{6,30},{7,31},{8,0},{9,1... | collective-permute-start | bytes 7864328 | tf_op jit(solution)/shard_map/ppermute | solution.py:24
  113.1 55.1 %copy-start.4 = (bf16[320,4096]{1,0:T(8,128)(2,1)}, bf16[320,4096]{1,0:T(8,128)(2,1)S(1)}, u32[]{:S(2)}) copy-start(bf16[320,4096]{1,0:T(8,128)(2,1)S(1)} %collective-permute-done.10.refs_1_) | copy-start | bytes 7864324
  114.4 42.5 %collective-permute-start.12 = (bf16[160,4096]{1,0:T(8,128)(2,1)}, bf16[160,4096]{1,0:T(8,128)(2,1)}, u32[]{:S(2)}, u32[]{:S(2)}) collective-permute-start(bf16[160,4096]{1,0:T(8,128)(2,1)} %slice.302), channel_id=1, source_target_pairs={{0,2},{1,3},{2,4},{3,5},{4,6},{5,7},{6,0},{7,1},{8,10},{9,11},{10,... | collective-permute-start | bytes 3932168 | tf_op jit(solution)/shard_map/ppermute | solution.py:24
  117.0 11.4 %copy-start.14 = (bf16[4096,448]{0,1:T(8,128)(2,1)S(1)}, bf16[4096,448]{0,1:T(8,128)(2,1)}, u32[]{:S(2)}) copy-start(bf16[4096,448]{0,1:T(8,128)(2,1)} %param.23) | copy-start | bytes 11010052
  117.0 39.9 %collective-permute-start.13 = (bf16[160,4096]{1,0:T(8,128)(2,1)}, bf16[160,4096]{1,0:T(8,128)(2,1)}, u32[]{:S(2)}, u32[]{:S(2)}) collective-permute-start(bf16[160,4096]{1,0:T(8,128)(2,1)} %slice.303), channel_id=1, source_target_pairs={{0,6},{1,7},{2,0},{3,1},{4,2},{5,3},{6,4},{7,5},{8,14},{9,15},{10,... | collective-permute-start | bytes 3932168 | tf_op jit(solution)/shard_map/ppermute | solution.py:24
  122.7 37.0 %collective-permute-start.18 = (bf16[160,4096]{1,0:T(8,128)(2,1)}, bf16[160,4096]{1,0:T(8,128)(2,1)}, u32[]{:S(2)}, u32[]{:S(2)}) collective-permute-start(bf16[160,4096]{1,0:T(8,128)(2,1)} %slice.316), channel_id=1, source_target_pairs={{0,8},{1,9},{2,10},{3,11},{4,12},{5,13},{6,14},{7,15},{8,16},{9,17... | collective-permute-start | bytes 3932168 | tf_op jit(solution)/shard_map/ppermute | solution.py:24
  126.7 33.1 %collective-permute-start.19 = (bf16[160,4096]{1,0:T(8,128)(2,1)}, bf16[160,4096]{1,0:T(8,128)(2,1)}, u32[]{:S(2)}, u32[]{:S(2)}) collective-permute-start(bf16[160,4096]{1,0:T(8,128)(2,1)} %slice.317), channel_id=1, source_target_pairs={{0,24},{1,25},{2,26},{3,27},{4,28},{5,29},{6,30},{7,31},{8,0},{9,1... | collective-permute-start | bytes 3932168 | tf_op jit(solution)/shard_map/ppermute | solution.py:24
  135.0 4.6 %copy-start.16 = (bf16[4096,448]{0,1:T(8,128)(2,1)S(1)}, bf16[4096,448]{0,1:T(8,128)(2,1)}, u32[]{:S(2)}) copy-start(bf16[4096,448]{0,1:T(8,128)(2,1)} %all-gather.3.cloned.1.call-done) | copy-start | bytes 11010052
  143.7 4.5 %copy-start.18 = (bf16[4096,448]{0,1:T(8,128)(2,1)S(1)}, bf16[4096,448]{0,1:T(8,128)(2,1)}, u32[]{:S(2)}) copy-start(bf16[4096,448]{0,1:T(8,128)(2,1)} %all-gather.5.cloned.1.call-done) | copy-start | bytes 11010052
  156.9 2.1 collective-permute-start.16
  159.0 3.1 %collective-permute-start.17 = (bf16[8,128]{1,0:T(8,128)(2,1)S(1)}, bf16[8,128]{1,0:T(8,128)(2,1)S(1)}, u32[]{:S(2)}, u32[]{:S(2)}) collective-permute-start(bf16[8,128]{1,0:T(8,128)(2,1)S(1)} %collective-permute-done.16), channel_id=1, source_target_pairs={{0,32},{32,0},{64,96},{96,64},{1,33},{33,1},{65,97},{97,65},{2,34}... | collective-permute-start | bytes 6152 | tf_op jit(solution)/shard_map/ppermute | solution.py:38
  177.5 37.4 %collective-permute-start.31 = (f32[2,448,1024]{2,1,0:T(8,128)}, f32[2,448,1024]{2,1,0:T(8,128)}, u32[]{:S(2)}, u32[]{:S(2)}) collective-permute-start(f32[2,448,1024]{2,1,0:T(8,128)} %get-tuple-element.102), channel_id=1, source_target_pairs={{0,32},{32,0},{64,96},{96,64},{1,33},{33,1},{65,97},{97,65},{2,34}... | collective-permute-start | bytes 11010056 | tf_op jit(solution)/shard_map/ppermute | solution.py:38
  177.5 42.4 %collective-permute-start.30 = (f32[2,448,1024]{2,1,0:T(8,128)}, f32[2,448,1024]{2,1,0:T(8,128)}, u32[]{:S(2)}, u32[]{:S(2)}) collective-permute-start(f32[2,448,1024]{2,1,0:T(8,128)} %get-tuple-element.99), channel_id=1, source_target_pairs={{0,32},{32,0},{64,96},{96,64},{1,33},{33,1},{65,97},{97,65},{2,34}... | collective-permute-start | bytes 11010056 | tf_op jit(solution)/shard_map/ppermute | solution.py:38
  179.8 13.0 %copy-start.19 = (s32[4]{0:T(128)S(1)}, s32[4]{0:T(128)}, u32[]{:S(2)}) copy-start(s32[4]{0:T(128)} %param.26) | copy-start | bytes 52
  179.8 64.6 %copy-start.3 = (bf16[2,1024,448]{1,2,0:T(8,128)(2,1)S(1)}, bf16[2,1024,448]{1,2,0:T(8,128)(2,1)}, u32[]{:S(2)}) copy-start(bf16[2,1024,448]{1,2,0:T(8,128)(2,1)} %param.27) | copy-start | bytes 5505028
  190.3 5.2 %collective-permute-start.20 = (f32[8,128]{1,0:T(8,128)S(1)}, f32[8,128]{1,0:T(8,128)S(1)}, u32[]{:S(2)}, u32[]{:S(2)}) collective-permute-start(f32[8,128]{1,0:T(8,128)S(1)} %broadcast_in_dim.9), channel_id=1, source_target_pairs={{0,1},{1,0},{2,3},{3,2},{4,5},{5,4},{6,7},{7,6},{8,9},{9,8},{10,11... | collective-permute-start | bytes 12296 | tf_op jit(solution)/shard_map/ppermute | solution.py:28
  192.5 1.2 collective-permute-start.21
  192.5 3.0 %collective-permute-start.22 = (f32[8,128]{1,0:T(8,128)S(1)}, f32[8,128]{1,0:T(8,128)S(1)}, u32[]{:S(2)}, u32[]{:S(2)}) collective-permute-start(f32[8,128]{1,0:T(8,128)S(1)} %broadcast_in_dim.9), channel_id=1, source_target_pairs={{0,33},{1,32},{2,35},{3,34},{4,37},{5,36},{6,39},{7,38},{8,41},{9,... | collective-permute-start | bytes 12296 | tf_op jit(solution)/shard_map/ppermute | solution.py:34
  196.2 6.0 %collective-permute-start.23 = (f32[16,128]{1,0:T(8,128)S(1)}, f32[16,128]{1,0:T(8,128)S(1)}, u32[]{:S(2)}, u32[]{:S(2)}) collective-permute-start(f32[16,128]{1,0:T(8,128)S(1)} %pad_maximum_fusion.3), channel_id=1, source_target_pairs={{0,8},{1,9},{2,10},{3,11},{4,12},{5,13},{6,14},{7,15},{8,0},{9,1},... | collective-permute-start | bytes 24584 | tf_op jit(solution)/shard_map/ppermute | solution.py:28
  196.7 5.6 %collective-permute-start.24 = (f32[16,128]{1,0:T(8,128)S(1)}, f32[16,128]{1,0:T(8,128)S(1)}, u32[]{:S(2)}, u32[]{:S(2)}) collective-permute-start(f32[16,128]{1,0:T(8,128)S(1)} %pad_maximum_fusion.3), channel_id=1, source_target_pairs={{0,16},{1,17},{2,18},{3,19},{4,20},{5,21},{6,22},{7,23},{8,24},{9,... | collective-permute-start | bytes 24584 | tf_op jit(solution)/shard_map/ppermute | solution.py:28
  199.4 4.9 %collective-permute-start.25 = (f32[16,128]{1,0:T(8,128)S(1)}, f32[16,128]{1,0:T(8,128)S(1)}, u32[]{:S(2)}, u32[]{:S(2)}) collective-permute-start(f32[16,128]{1,0:T(8,128)S(1)} %pad_maximum_fusion.3), channel_id=1, source_target_pairs={{0,24},{1,25},{2,26},{3,27},{4,28},{5,29},{6,30},{7,31},{8,16},{9,... | collective-permute-start | bytes 24584 | tf_op jit(solution)/shard_map/ppermute | solution.py:28
  204.2 6.2 %collective-permute-start.26 = (f32[16,128]{1,0:T(8,128)S(1)}, f32[16,128]{1,0:T(8,128)S(1)}, u32[]{:S(2)}, u32[]{:S(2)}) collective-permute-start(f32[16,128]{1,0:T(8,128)S(1)} %add_add_fusion), channel_id=1, source_target_pairs={{0,2},{1,3},{2,0},{3,1},{4,6},{5,7},{6,4},{7,5},{8,10},{9,11},{10,... | collective-permute-start | bytes 24584 | tf_op jit(solution)/shard_map/ppermute | solution.py:28
  204.2 6.2 %collective-permute-start.27 = (f32[16,128]{1,0:T(8,128)S(1)}, f32[16,128]{1,0:T(8,128)S(1)}, u32[]{:S(2)}, u32[]{:S(2)}) collective-permute-start(f32[16,128]{1,0:T(8,128)S(1)} %add_add_fusion), channel_id=1, source_target_pairs={{0,4},{1,5},{2,6},{3,7},{4,0},{5,1},{6,2},{7,3},{8,12},{9,13},{10,... | collective-permute-start | bytes 24584 | tf_op jit(solution)/shard_map/ppermute | solution.py:28
  205.8 4.9 %collective-permute-start.28 = (f32[16,128]{1,0:T(8,128)S(1)}, f32[16,128]{1,0:T(8,128)S(1)}, u32[]{:S(2)}, u32[]{:S(2)}) collective-permute-start(f32[16,128]{1,0:T(8,128)S(1)} %add_add_fusion), channel_id=1, source_target_pairs={{0,6},{1,7},{2,4},{3,5},{4,2},{5,3},{6,0},{7,1},{8,14},{9,15},{10,... | collective-permute-start | bytes 24584 | tf_op jit(solution)/shard_map/ppermute | solution.py:28
  210.4 9.5 %copy-start.2 = (f32[2,448,1024]{2,1,0:T(8,128)S(1)}, f32[2,448,1024]{2,1,0:T(8,128)}, u32[]{:S(2)}) copy-start(f32[2,448,1024]{2,1,0:T(8,128)} %get-tuple-element.98.keep) | copy-start | bytes 11010052
  211.3 16.0 %collective-permute-start.29 = (f32[8,128]{1,0:T(8,128)S(1)}, f32[8,128]{1,0:T(8,128)S(1)}, u32[]{:S(2)}, u32[]{:S(2)}) collective-permute-start(f32[8,128]{1,0:T(8,128)S(1)} %fusion.18), channel_id=1, source_target_pairs={{0,64},{32,96},{64,0},{96,32},{1,65},{33,97},{65,1},{97,33},{2,66}... | collective-permute-start | bytes 12296 | tf_op jit(solution)/shard_map/ppermute | solution.py:42
  219.3 24.9 %collective-permute-start.32 = (f16[448,1024]{1,0:T(8,128)(2,1)S(1)}, f16[448,1024]{1,0:T(8,128)(2,1)S(1)}, u32[]{:S(2)}, u32[]{:S(2)}) collective-permute-start(f16[448,1024]{1,0:T(8,128)(2,1)S(1)} %fusion.6), channel_id=1, source_target_pairs={{0,64},{32,96},{64,0},{96,32},{1,65},{33,97},{65,1},{97,33},{2,66}... | collective-permute-start | bytes 2752520 | tf_op jit(solution)/shard_map/ppermute | solution.py:42
  219.9 24.5 %copy-start.1 = (f32[2,1024,448]{1,2,0:T(8,128)S(1)}, f32[2,1024,448]{1,2,0:T(8,128)}, u32[]{:S(2)}) copy-start(f32[2,1024,448]{1,2,0:T(8,128)} %param.29) | copy-start | bytes 11010052
  223.3 21.0 %copy-start = (f32[2,1024,448]{1,2,0:T(8,128)S(1)}, f32[2,1024,448]{1,2,0:T(8,128)}, u32[]{:S(2)}) copy-start(f32[2,1024,448]{1,2,0:T(8,128)} %param.28) | copy-start | bytes 11010052
  227.0 1.5 collective-permute-start.33
  228.5 3.2 %collective-permute-start.34 = (f32[8,128]{1,0:T(8,128)S(1)}, f32[8,128]{1,0:T(8,128)S(1)}, u32[]{:S(2)}, u32[]{:S(2)}) collective-permute-start(f32[8,128]{1,0:T(8,128)S(1)} %collective-permute-done.33), channel_id=1, source_target_pairs={{0,32},{32,0},{64,96},{96,64},{1,33},{33,1},{65,97},{97,65},{2,34}... | collective-permute-start | bytes 12296 | tf_op jit(solution)/shard_map/ppermute | solution.py:38
  228.7 25.5 %collective-permute-start.36 = (f16[256,1024]{1,0:T(8,128)(2,1)S(1)}, f16[256,1024]{1,0:T(8,128)(2,1)S(1)}, u32[]{:S(2)}, u32[]{:S(2)}) collective-permute-start(f16[256,1024]{1,0:T(8,128)(2,1)S(1)} %fusion.10), channel_id=1, source_target_pairs={{0,64},{32,96},{64,0},{96,32},{1,65},{33,97},{65,1},{97,33},{2,66}... | collective-permute-start | bytes 1572872 | tf_op jit(solution)/shard_map/ppermute | solution.py:42
  253.5 9.4 %collective-permute-start.35 = (f16[192,1024]{1,0:T(8,128)(2,1)S(1)}, f16[192,1024]{1,0:T(8,128)(2,1)S(1)}, u32[]{:S(2)}, u32[]{:S(2)}) collective-permute-start(f16[192,1024]{1,0:T(8,128)(2,1)S(1)} %fusion.34), channel_id=1, source_target_pairs={{0,64},{32,96},{64,0},{96,32},{1,65},{33,97},{65,1},{97,33},{2,66}... | collective-permute-start | bytes 1179656 | tf_op jit(solution)/shard_map/ppermute | solution.py:42
  (11 other events, 25.9 us)
Sparse Core Ops, SparseCore 0:
  9.7 38.7 all-gather.2
  50.2 35.3 all-gather.4

commit v2 on v1

--- a/solution.py
+++ b/solution.py
@@ -240,7 +240,7 @@
         total = (w_own * kept[1, rows] + w_other * received[1, rows]) * scale
         return total.astype(jnp.float16)
 
-    cut = 256
+    cut = 320
     turn = lambda a: a.transpose(0, 2, 1)
     states = [turn(a) for a in (noise, first_moment, second_moment)]
     up_arrived = swap_far(weighted(up_kept, up_received, slice(None)))

time: 275 us -> 273 us (level)
  transfers between devices with their start and end apart: 39 -> 39, of which waited for: 12 -> 12; matrix products, arithmetic and copies ran while one was open for 31% -> 31% of each run, Pallas kernels for 7% -> 8%
where the time goes in v2:
time: 273 us; the launch traced here: 272 us
  waiting for transfers between devices  79.9 us (29%)
  starting transfers between devices  51 us (19%)
  matrix products  37.2 us (14%)
  Pallas kernels  33.2 us (12%)
  local copies, waits for them, and re-layouts  31.9 us (12%)
  other arithmetic  24 us (9%)
  between operations  14.5 us (5%)
    ppermute x18, waiting for transfers between devices, send(): lax.ppermute(value, 'mp', pairs(lambda x, z, y: (x + dx, z + dz, y + dy)))  57.9 us
    dot_general x12, matrix products, rows_dot(): lax.dot_general(rows, weight, (((1,), (0,)), ((), ())), preferred_element...  37.2 us
    ppermute x18, starting transfers between devices, send(): lax.ppermute(value, 'mp', pairs(lambda x, z, y: (x + dx, z + dz, y + dy)))  30 us
    pallas_call x2, Pallas kernels, deltas(): pl.pallas_call(kernel, grid_spec=pltpu.PrefetchScalarGridSpec(num_scalar_...  18.6 us
    ppermute x4, waiting for transfers between devices, swap_far(): return lax.ppermute(value, 'client', [(c, c ^ 2) for c in range(4)])  15.7 us
    unnamed x49, local copies, waits for them, and re-layouts  15 us
    pallas_call x3, Pallas kernels, adam(): pl.pallas_call(kernel, grid=(units // block,), in_specs=[pl.BlockSpec((24...  13.8 us
    slice x8, local copies, waits for them, and re-layouts, ring(): return [block, below, above, below[:half], above[half:]]  11.9 us
  transfers between devices with their start and end apart: 39, of which 12 were waited for; matrix products, arithmetic and copies ran while one was open for 31% of the time, Pallas kernels for 8%

profile of v2, /device:TPU:0, one launch (start us, length us, event | category | flops | bytes accessed | tf_op | source)
XLA Modules:
  0.0 271.7 jit_solution(6750137740439712502)
XLA Ops:
  7.9 1.7 collective-permute-start
  10.0 1.9 constant_dynamic-update-slice_fusion.1
  11.9 1.7 constant_dynamic-update-slice_fusion.15
  13.7 5.2 %collective-permute-done = bf16[40,4096]{1,0:T(8,128)(2,1)S(1)} collective-permute-done((bf16[40,4096]{1,0:T(8,128)(2,1)}, bf16[40,4096]{1,0:T(8,128)(2,1)S(1)}, u32[]{:S(2)}, u32[]{:S(2)}) %collective-permute-start) | collective-permute-done | bytes 327712 | tf_op jit(solution)/shard_map/ppermute | solution.py:24
  23.0 3.0 %collective-permute-done.5 = bf16[40,4096]{1,0:T(8,128)(2,1)S(1)} collective-permute-done((bf16[40,4096]{1,0:T(8,128)(2,1)}, bf16[40,4096]{1,0:T(8,128)(2,1)S(1)}, u32[]{:S(2)}, u32[]{:S(2)}) %collective-permute-start.5) | collective-permute-done | bytes 327712 | tf_op jit(solution)/shard_map/ppermute | solution.py:24
  26.8 2.1 collective-permute-start.6
  28.9 2.9 %collective-permute-start.8 = (bf16[80,4096]{1,0:T(8,128)(2,1)}, bf16[80,4096]{1,0:T(8,128)(2,1)}, u32[]{:S(2)}, u32[]{:S(2)}) collective-permute-start(bf16[80,4096]{1,0:T(8,128)(2,1)} %get-tuple-element.116), channel_id=1, source_target_pairs={{0,6},{1,7},{2,0},{3,1},{4,2},{5,3},{6,4},{7,5},{8,14},{9,15},{10,... | collective-permute-start | bytes 1966088 | tf_op jit(solution)/shard_map/ppermute | solution.py:24
  31.8 3.7 %collective-permute-done.1 = bf16[80,4096]{1,0:T(8,128)(2,1)S(1)} collective-permute-done((bf16[80,4096]{1,0:T(8,128)(2,1)}, bf16[80,4096]{1,0:T(8,128)(2,1)S(1)}, u32[]{:S(2)}, u32[]{:S(2)}) %collective-permute-start.1) | collective-permute-done | bytes 655392 | tf_op jit(solution)/shard_map/ppermute | solution.py:24
  37.3 2.6 collective-permute-start.4
  39.9 3.9 %collective-permute-done.6 = bf16[80,4096]{1,0:T(8,128)(2,1)} collective-permute-done((bf16[80,4096]{1,0:T(8,128)(2,1)}, bf16[80,4096]{1,0:T(8,128)(2,1)}, u32[]{:S(2)}, u32[]{:S(2)}) %collective-permute-start.6) | collective-permute-done | bytes 655392 | tf_op jit(solution)/shard_map/ppermute | solution.py:24
  45.9 3.3 %collective-permute-start.9 = (bf16[40,4096]{1,0:T(8,128)(2,1)S(1)}, bf16[40,4096]{1,0:T(8,128)(2,1)S(1)}, u32[]{:S(2)}, u32[]{:S(2)}) collective-permute-start(bf16[40,4096]{1,0:T(8,128)(2,1)S(1)} %slice.300), channel_id=1, source_target_pairs={{0,6},{1,7},{2,0},{3,1},{4,2},{5,3},{6,4},{7,5},{8,14},{9,15},{10,... | collective-permute-start | bytes 983048 | tf_op jit(solution)/shard_map/ppermute | solution.py:24
  50.0 2.0 constant_dynamic-update-slice_fusion.4
  57.3 3.2 %collective-permute-start.11 = (bf16[320,4096]{1,0:T(8,128)(2,1)}, bf16[320,4096]{1,0:T(8,128)(2,1)}, u32[]{:S(2)}, u32[]{:S(2)}) collective-permute-start(bf16[320,4096]{1,0:T(8,128)(2,1)} %fusion.32.refs_0_), channel_id=1, source_target_pairs={{0,6},{1,7},{2,0},{3,1},{4,2},{5,3},{6,4},{7,5},{8,14},{9,15},{10,... | collective-permute-start | bytes 7864328 | tf_op jit(solution)/shard_map/ppermute | solution.py:24
  64.8 1.7 collective-permute-start.15
  66.7 4.4 %fusion.38.refs_0_ = f32[320,448]{1,0:T(8,128)S(1)} fusion(bf16[320,4096]{1,0:T(8,128)(2,1)} %fusion.32.refs_0_, bf16[4096,448]{0,1:T(8,128)(2,1)} %param.23), kind=kOutput, calls=%fused_computation.96 | convolution fusion | flops 1174405120 | bytes 6864896 | tf_op jit(solution)/shard_map/dot_general | solution.py:77
  71.1 42.1 %collective-permute-done.10.refs_1_ = bf16[320,4096]{1,0:T(8,128)(2,1)S(1)} collective-permute-done((bf16[320,4096]{1,0:T(8,128)(2,1)}, bf16[320,4096]{1,0:T(8,128)(2,1)S(1)}, u32[]{:S(2)}, u32[]{:S(2)}) %collective-permute-start.10) | collective-permute-done | bytes 2621472 | tf_op jit(solution)/shard_map/ppermute | solution.py:24
  114.4 2.6 slice.303
  117.0 3.2 %collective-permute-start.13 = (bf16[160,4096]{1,0:T(8,128)(2,1)}, bf16[160,4096]{1,0:T(8,128)(2,1)}, u32[]{:S(2)}, u32[]{:S(2)}) collective-permute-start(bf16[160,4096]{1,0:T(8,128)(2,1)} %slice.303), channel_id=1, source_target_pairs={{0,6},{1,7},{2,0},{3,1},{4,2},{5,3},{6,4},{7,5},{8,14},{9,15},{10,... | collective-permute-start | bytes 3932168 | tf_op jit(solution)/shard_map/ppermute | solution.py:24
  120.2 2.5 slice.316
  124.2 2.5 slice.317
  126.7 1.8 collective-permute-start.19
  128.5 2.4 fusion.39.refs_3_
  130.9 4.1 %fusion.40.refs_6_ = f32[320,448]{1,0:T(8,128)} fusion(bf16[320,4096]{1,0:T(8,128)(2,1)} %collective-permute-done.11.refs_2_, bf16[4096,448]{0,1:T(8,128)(2,1)S(1)} %copy-done.14), kind=kOutput, calls=%fused_computation.98 | convolution fusion | flops 1174405120 | bytes 6864896 | tf_op jit(solution)/shard_map/dot_general | solution.py:77
  135.0 4.6 %fusion.42.refs_4_ = f32[320,448]{1,0:T(8,128)} fusion(bf16[320,4096]{1,0:T(8,128)(2,1)S(1)} %collective-permute-done.10.refs_1_, bf16[4096,448]{0,1:T(8,128)(2,1)} %all-gather.3.cloned.1.call-done), kind=kOutput, calls=%fused_computation.100 | convolution fusion | flops 1174405120 | bytes 6864896 | tf_op jit(solution)/shard_map/dot_general | solution.py:77
  139.6 4.2 %fusion.43.refs_7_ = f32[320,448]{1,0:T(8,128)} fusion(bf16[320,4096]{1,0:T(8,128)(2,1)} %collective-permute-done.11.refs_2_, bf16[4096,448]{0,1:T(8,128)(2,1)S(1)} %copy-done.16), kind=kOutput, calls=%fused_computation.101 | convolution fusion | flops 1174405120 | bytes 6864896 | tf_op jit(solution)/shard_map/dot_general | solution.py:77
  143.7 4.5 %fusion.45.refs_5_ = f32[320,448]{1,0:T(8,128)S(1)} fusion(bf16[320,4096]{1,0:T(8,128)(2,1)} %collective-permute-done.14.refs_5_, bf16[4096,448]{0,1:T(8,128)(2,1)} %all-gather.5.cloned.1.call-done), kind=kOutput, calls=%fused_computation.103 | convolution fusion | flops 1174405120 | bytes 6864896 | tf_op jit(solution)/shard_map/dot_general | solution.py:77
  148.3 3.4 %fusion.46.refs_8_ = f32[320,448]{1,0:T(8,128)S(1)} fusion(bf16[320,4096]{1,0:T(8,128)(2,1)} %collective-permute-done.15.refs_6_, bf16[4096,448]{0,1:T(8,128)(2,1)S(1)} %copy-done.18), kind=kOutput, calls=%fused_computation.104 | convolution fusion | flops 1174405120 | bytes 6864896 | tf_op jit(solution)/shard_map/dot_general | solution.py:77
  151.7 3.4 %fusion.41.refs_1_ = f32[320,448]{1,0:T(8,128)S(1)} fusion(bf16[320,4096]{1,0:T(8,128)(2,1)} %fusion.32.refs_0_, bf16[4096,448]{0,1:T(8,128)(2,1)S(1)} %copy-done.17), kind=kOutput, calls=%fused_computation.99 | convolution fusion | flops 1174405120 | bytes 6864896 | tf_op jit(solution)/shard_map/dot_general | solution.py:77
  157.0 2.0 pad_maximum_fusion
  159.8 2.3 pad_maximum_fusion.1
  168.2 9.3 %shard_map.113 = (f32[2,448,1024]{2,1,0:T(8,128)}, f32[2,448,1024]{2,1,0:T(8,128)}, f32[8,128]{1,0:T(8,128)S(1)}) custom-call(s32[2]{0:T(128)S(1)} %get-tuple-element.130._, bf16[320,4096]{1,0:T(8,128)(2,1)} %fusion.32.refs_0_, bf16[320,4096]{1,0:T(8,128)(2,1)S(1)} %collective-permute-done.10.refs_1_, bf16[320,4096]{1,0:T(8,128)(2,1)} %collective-permute-done.11.refs_2_, ...), custom_call_target="tpu_custom_call" | custom-call | flops 4697620480 | bytes 17825792 | tf_op jit(solution)/shard_map/pallas_call | solution.py:127
  179.8 9.3 %shard_map.114 = (f32[2,448,1024]{2,1,0:T(8,128)}, f32[2,448,1024]{2,1,0:T(8,128)}, f32[8,128]{1,0:T(8,128)S(1)}) custom-call(s32[2]{0:T(128)S(1)} %get-tuple-element.129._, bf16[320,4096]{1,0:T(8,128)(2,1)} %fusion.32.refs_0_, bf16[320,4096]{1,0:T(8,128)(2,1)S(1)} %copy-done.5, bf16[320,4096]{1,0:T(8,128)(2,1)} %collective-permute-done.11.refs_2_, ...), custom_call_target="tpu_custom_call" | custom-call | flops 4697620480 | bytes 17825792 | tf_op jit(solution)/shard_map/pallas_call | solution.py:127
  190.3 2.2 collective-permute-start.20
  193.7 1.9 collective-permute-done.22
  196.7 2.7 collective-permute-start.24
  202.2 2.0 collective-permute-done.25
  205.8 3.1 %collective-permute-start.28 = (f32[16,128]{1,0:T(8,128)S(1)}, f32[16,128]{1,0:T(8,128)S(1)}, u32[]{:S(2)}, u32[]{:S(2)}) collective-permute-start(f32[16,128]{1,0:T(8,128)S(1)} %add_add_fusion), channel_id=1, source_target_pairs={{0,6},{1,7},{2,4},{3,5},{4,2},{5,3},{6,0},{7,1},{8,14},{9,15},{10,... | collective-permute-start | bytes 24584 | tf_op jit(solution)/shard_map/ppermute | solution.py:28
  211.3 3.0 %collective-permute-start.29 = (f32[8,128]{1,0:T(8,128)S(1)}, f32[8,128]{1,0:T(8,128)S(1)}, u32[]{:S(2)}, u32[]{:S(2)}) collective-permute-start(f32[8,128]{1,0:T(8,128)S(1)} %fusion.18), channel_id=1, source_target_pairs={{0,64},{32,96},{64,0},{96,32},{1,65},{33,97},{65,1},{97,33},{2,66}... | collective-permute-start | bytes 12296 | tf_op jit(solution)/shard_map/ppermute | solution.py:42
  214.9 4.4 %fusion.6 = f16[448,1024]{1,0:T(8,128)(2,1)S(1)} fusion(f32[2,448,1024]{2,1,0:T(8,128)} %collective-permute-done.31.received, f32[2,448,1024]{2,1,0:T(8,128)} %get-tuple-element.101.keep, f32[]{:T(128)} %bitcast.4, f32[]{:T(128)} %bitcast.3, f32[]{:T(128)} %bitcast.2), kind=kLoop, calls=%fused_computation.10 | loop fusion | flops 2293760 | bytes 4587532 | tf_op jit(solution)/shard_map/convert_element_type | solution.py:241
  219.9 3.3 %fusion.11 = f16[128,1024]{1,0:T(8,128)(2,1)S(1)} fusion(f32[2,448,1024]{2,1,0:T(8,128)} %collective-permute-done.30.received, f32[2,448,1024]{2,1,0:T(8,128)S(1)} %copy-done.2, f32[]{:T(128)} %bitcast.4, f32[]{:T(128)} %bitcast.3, f32[]{:T(128)} %bitcast.2), kind=kLoop, calls=%fused_computation.16 | loop fusion | flops 655360 | bytes 1310732 | tf_op jit(solution)/shard_map/convert_element_type | solution.py:241
  223.2 3.8 %fusion.7 = f16[320,1024]{1,0:T(8,128)(2,1)S(1)} fusion(f32[2,448,1024]{2,1,0:T(8,128)} %collective-permute-done.30.received, f32[2,448,1024]{2,1,0:T(8,128)S(1)} %copy-done.2, f32[]{:T(128)} %bitcast.4, f32[]{:T(128)} %bitcast.3, f32[]{:T(128)} %bitcast.2), kind=kLoop, calls=%fused_computation.11 | loop fusion | flops 1638400 | bytes 3276812 | tf_op jit(solution)/shard_map/convert_element_type | solution.py:241
  228.7 3.0 %collective-permute-start.36 = (f16[320,1024]{1,0:T(8,128)(2,1)S(1)}, f16[320,1024]{1,0:T(8,128)(2,1)S(1)}, u32[]{:S(2)}, u32[]{:S(2)}) collective-permute-start(f16[320,1024]{1,0:T(8,128)(2,1)S(1)} %fusion.7), channel_id=1, source_target_pairs={{0,64},{32,96},{64,0},{96,32},{1,65},{33,97},{65,1},{97,33},{2,66}... | collective-permute-start | bytes 1966088 | tf_op jit(solution)/shard_map/ppermute | solution.py:42
  231.7 12.5 %collective-permute-done.32 = f16[448,1024]{1,0:T(8,128)(2,1)S(1)} collective-permute-done((f16[448,1024]{1,0:T(8,128)(2,1)S(1)}, f16[448,1024]{1,0:T(8,128)(2,1)S(1)}, u32[]{:S(2)}, u32[]{:S(2)}) %collective-permute-start.32) | collective-permute-done | bytes 917536 | tf_op jit(solution)/shard_map/ppermute | solution.py:42
  244.4 2.0 copy-done.6
  246.4 6.4 %shard_map.115 = (f32[2,448,1024]{2,1,0:T(8,128)}, f32[2,448,1024]{2,1,0:T(8,128)}, f32[2,448,1024]{2,1,0:T(8,128)}) custom-call(f32[24,128]{1,0:T(8,128)S(1)} %pad_maximum_fusion.2.factors, f32[2,448,1024]{2,1,0:T(8,128)S(1)} %copy-done.6, f32[2,448,1024]{2,1,0:T(8,128)} %collective-permute-done.31.received, f32[448,1024]{1,0:T(8,128)S(1)} %convert_element_type.67.arrived, ...), custom_call_target="tpu_custom_call" | custom-call | flops 5505024 | bytes 15597568 | tf_op jit(solution)/shard_map/pallas_call | solution.py:163
  254.1 3.2 %collective-permute-done.36 = f16[320,1024]{1,0:T(8,128)(2,1)S(1)} collective-permute-done((f16[320,1024]{1,0:T(8,128)(2,1)S(1)}, f16[320,1024]{1,0:T(8,128)(2,1)S(1)}, u32[]{:S(2)}, u32[]{:S(2)}) %collective-permute-start.36) | collective-permute-done | bytes 655392 | tf_op jit(solution)/shard_map/ppermute | solution.py:42
  257.5 5.0 %shard_map.116 = (f32[2,448,1024]{2,1,0:T(8,128)}, f32[2,448,1024]{2,1,0:T(8,128)}, f32[2,448,1024]{2,1,0:T(8,128)}) custom-call(f32[24,128]{1,0:T(8,128)S(1)} %pad_maximum_fusion.2.factors, f32[2,448,1024]{2,1,0:T(8,128)S(1)} %copy-done.2, ...), custom_call_target="tpu_custom_call", output_to_operand_aliasing={{0}: (7, {}), {1}: (8, {}), {2}: (9, {})} | custom-call | flops 3932160 | bytes 11141120 | tf_op jit(solution)/shard_map/pallas_call | solution.py:163
  262.5 2.4 shard_map.117
  (148 shorter events, 49.0 us)
Async XLA Ops:
  7.2 127.8 %all-gather.3.cloned.1.call-start = ((), (), s32[]{:S(2)}) async-start(), calls=%async_computation | async-start | bytes 4587520 | tf_op jit(solution)/shard_map/all_gather | solution.py:193
  7.9 135.8 %all-gather.5.cloned.1.call-start = ((), (), s32[]{:S(2)}) async-start(), calls=%async_computation.1 | async-start | bytes 4587520 | tf_op jit(solution)/shard_map/all_gather | solution.py:194
  7.9 10.9 %collective-permute-start = (bf16[40,4096]{1,0:T(8,128)(2,1)}, bf16[40,4096]{1,0:T(8,128)(2,1)S(1)}, u32[]{:S(2)}, u32[]{:S(2)}) collective-permute-start(bf16[40,4096]{1,0:T(8,128)(2,1)} %param.21), channel_id=1, source_target_pairs={{0,1},{1,0},{2,3},{3,2},{4,5},{5,4},{6,7},{7,6},{8,9},{9,8},{10,11... | collective-permute-start | bytes 983048 | tf_op jit(solution)/shard_map/ppermute | solution.py:24
  9.7 16.3 %collective-permute-start.5 = (bf16[40,4096]{1,0:T(8,128)(2,1)}, bf16[40,4096]{1,0:T(8,128)(2,1)S(1)}, u32[]{:S(2)}, u32[]{:S(2)}) collective-permute-start(bf16[40,4096]{1,0:T(8,128)(2,1)} %param.22), channel_id=1, source_target_pairs={{0,1},{1,0},{2,3},{3,2},{4,5},{5,4},{6,7},{7,6},{8,9},{9,8},{10,11... | collective-permute-start | bytes 983048 | tf_op jit(solution)/shard_map/ppermute | solution.py:24
  19.7 15.7 %collective-permute-start.1 = (bf16[80,4096]{1,0:T(8,128)(2,1)}, bf16[80,4096]{1,0:T(8,128)(2,1)S(1)}, u32[]{:S(2)}, u32[]{:S(2)}) collective-permute-start(bf16[80,4096]{1,0:T(8,128)(2,1)} %get-tuple-element.119), channel_id=1, source_target_pairs={{0,8},{1,9},{2,10},{3,11},{4,12},{5,13},{6,14},{7,15},{8,16},{9,17... | collective-permute-start | bytes 1966088 | tf_op jit(solution)/shard_map/ppermute | solution.py:24
  21.3 15.0 %collective-permute-start.2 = (bf16[80,4096]{1,0:T(8,128)(2,1)}, bf16[80,4096]{1,0:T(8,128)(2,1)}, u32[]{:S(2)}, u32[]{:S(2)}) collective-permute-start(bf16[80,4096]{1,0:T(8,128)(2,1)} %get-tuple-element.119), channel_id=1, source_target_pairs={{0,24},{1,25},{2,26},{3,27},{4,28},{5,29},{6,30},{7,31},{8,0},{9,1... | collective-permute-start | bytes 1966088 | tf_op jit(solution)/shard_map/ppermute | solution.py:24
  26.8 17.0 %collective-permute-start.6 = (bf16[80,4096]{1,0:T(8,128)(2,1)}, bf16[80,4096]{1,0:T(8,128)(2,1)}, u32[]{:S(2)}, u32[]{:S(2)}) collective-permute-start(bf16[80,4096]{1,0:T(8,128)(2,1)} %get-tuple-element.116), channel_id=1, source_target_pairs={{0,2},{1,3},{2,4},{3,5},{4,6},{5,7},{6,0},{7,1},{8,10},{9,11},{10,... | collective-permute-start | bytes 1966088 | tf_op jit(solution)/shard_map/ppermute | solution.py:24
  28.9 15.9 %collective-permute-start.8 = (bf16[80,4096]{1,0:T(8,128)(2,1)}, bf16[80,4096]{1,0:T(8,128)(2,1)}, u32[]{:S(2)}, u32[]{:S(2)}) collective-permute-start(bf16[80,4096]{1,0:T(8,128)(2,1)} %get-tuple-element.116), channel_id=1, source_target_pairs={{0,6},{1,7},{2,0},{3,1},{4,2},{5,3},{6,4},{7,5},{8,14},{9,15},{10,... | collective-permute-start | bytes 1966088 | tf_op jit(solution)/shard_map/ppermute | solution.py:24
  35.5 18.8 %collective-permute-start.3 = (bf16[40,4096]{1,0:T(8,128)(2,1)S(1)}, bf16[40,4096]{1,0:T(8,128)(2,1)S(1)}, u32[]{:S(2)}, u32[]{:S(2)}) collective-permute-start(bf16[40,4096]{1,0:T(8,128)(2,1)S(1)} %slice.296), channel_id=1, source_target_pairs={{0,8},{1,9},{2,10},{3,11},{4,12},{5,13},{6,14},{7,15},{8,16},{9,17... | collective-permute-start | bytes 983048 | tf_op jit(solution)/shard_map/ppermute | solution.py:24
  37.3 17.8 %collective-permute-start.4 = (bf16[40,4096]{1,0:T(8,128)(2,1)S(1)}, bf16[40,4096]{1,0:T(8,128)(2,1)S(1)}, u32[]{:S(2)}, u32[]{:S(2)}) collective-permute-start(bf16[40,4096]{1,0:T(8,128)(2,1)S(1)} %slice.297), channel_id=1, source_target_pairs={{0,24},{1,25},{2,26},{3,27},{4,28},{5,29},{6,30},{7,31},{8,0},{9,1... | collective-permute-start | bytes 983048 | tf_op jit(solution)/shard_map/ppermute | solution.py:24
  44.8 11.3 %collective-permute-start.7 = (bf16[40,4096]{1,0:T(8,128)(2,1)S(1)}, bf16[40,4096]{1,0:T(8,128)(2,1)S(1)}, u32[]{:S(2)}, u32[]{:S(2)}) collective-permute-start(bf16[40,4096]{1,0:T(8,128)(2,1)S(1)} %slice.298), channel_id=1, source_target_pairs={{0,2},{1,3},{2,4},{3,5},{4,6},{5,7},{6,0},{7,1},{8,10},{9,11},{10,... | collective-permute-start | bytes 983048 | tf_op jit(solution)/shard_map/ppermute | solution.py:24
  45.9 10.1 %collective-permute-start.9 = (bf16[40,4096]{1,0:T(8,128)(2,1)S(1)}, bf16[40,4096]{1,0:T(8,128)(2,1)S(1)}, u32[]{:S(2)}, u32[]{:S(2)}) collective-permute-start(bf16[40,4096]{1,0:T(8,128)(2,1)S(1)} %slice.300), channel_id=1, source_target_pairs={{0,6},{1,7},{2,0},{3,1},{4,2},{5,3},{6,4},{7,5},{8,14},{9,15},{10,... | collective-permute-start | bytes 983048 | tf_op jit(solution)/shard_map/ppermute | solution.py:24
  57.3 55.8 %collective-permute-start.10 = (bf16[320,4096]{1,0:T(8,128)(2,1)}, bf16[320,4096]{1,0:T(8,128)(2,1)S(1)}, u32[]{:S(2)}, u32[]{:S(2)}) collective-permute-start(bf16[320,4096]{1,0:T(8,128)(2,1)} %fusion.32.refs_0_), channel_id=1, source_target_pairs={{0,2},{1,3},{2,4},{3,5},{4,6},{5,7},{6,0},{7,1},{8,10},{9,11},{10,... | collective-permute-start | bytes 7864328 | tf_op jit(solution)/shard_map/ppermute | solution.py:24
  57.3 57.1 %collective-permute-start.11 = (bf16[320,4096]{1,0:T(8,128)(2,1)}, bf16[320,4096]{1,0:T(8,128)(2,1)}, u32[]{:S(2)}, u32[]{:S(2)}) collective-permute-start(bf16[320,4096]{1,0:T(8,128)(2,1)} %fusion.32.refs_0_), channel_id=1, source_target_pairs={{0,6},{1,7},{2,0},{3,1},{4,2},{5,3},{6,4},{7,5},{8,14},{9,15},{10,... | collective-permute-start | bytes 7864328 | tf_op jit(solution)/shard_map/ppermute | solution.py:24
  63.4 56.9 %collective-permute-start.14 = (bf16[320,4096]{1,0:T(8,128)(2,1)}, bf16[320,4096]{1,0:T(8,128)(2,1)}, u32[]{:S(2)}, u32[]{:S(2)}) collective-permute-start(bf16[320,4096]{1,0:T(8,128)(2,1)} %fusion.33.refs_4_), channel_id=1, source_target_pairs={{0,8},{1,9},{2,10},{3,11},{4,12},{5,13},{6,14},{7,15},{8,16},{9,17... | collective-permute-start | bytes 7864328 | tf_op jit(solution)/shard_map/ppermute | solution.py:24
  64.8 59.3 %collective-permute-start.15 = (bf16[320,4096]{1,0:T(8,128)(2,1)}, bf16[320,4096]{1,0:T(8,128)(2,1)}, u32[]{:S(2)}, u32[]{:S(2)}) collective-permute-start(bf16[320,4096]{1,0:T(8,128)(2,1)} %fusion.33.refs_4_), channel_id=1, source_target_pairs={{0,24},{1,25},{2,26},{3,27},{4,28},{5,29},{6,30},{7,31},{8,0},{9,1... | collective-permute-start | bytes 7864328 | tf_op jit(solution)/shard_map/ppermute | solution.py:24
  113.1 55.1 %copy-start.4 = (bf16[320,4096]{1,0:T(8,128)(2,1)}, bf16[320,4096]{1,0:T(8,128)(2,1)S(1)}, u32[]{:S(2)}) copy-start(bf16[320,4096]{1,0:T(8,128)(2,1)S(1)} %collective-permute-done.10.refs_1_) | copy-start | bytes 7864324
  114.4 42.5 %collective-permute-start.12 = (bf16[160,4096]{1,0:T(8,128)(2,1)}, bf16[160,4096]{1,0:T(8,128)(2,1)}, u32[]{:S(2)}, u32[]{:S(2)}) collective-permute-start(bf16[160,4096]{1,0:T(8,128)(2,1)} %slice.302), channel_id=1, source_target_pairs={{0,2},{1,3},{2,4},{3,5},{4,6},{5,7},{6,0},{7,1},{8,10},{9,11},{10,... | collective-permute-start | bytes 3932168 | tf_op jit(solution)/shard_map/ppermute | solution.py:24
  117.0 11.4 %copy-start.14 = (bf16[4096,448]{0,1:T(8,128)(2,1)S(1)}, bf16[4096,448]{0,1:T(8,128)(2,1)}, u32[]{:S(2)}) copy-start(bf16[4096,448]{0,1:T(8,128)(2,1)} %param.23) | copy-start | bytes 11010052
  117.0 39.9 %collective-permute-start.13 = (bf16[160,4096]{1,0:T(8,128)(2,1)}, bf16[160,4096]{1,0:T(8,128)(2,1)}, u32[]{:S(2)}, u32[]{:S(2)}) collective-permute-start(bf16[160,4096]{1,0:T(8,128)(2,1)} %slice.303), channel_id=1, source_target_pairs={{0,6},{1,7},{2,0},{3,1},{4,2},{5,3},{6,4},{7,5},{8,14},{9,15},{10,... | collective-permute-start | bytes 3932168 | tf_op jit(solution)/shard_map/ppermute | solution.py:24
  122.7 37.0 %collective-permute-start.18 = (bf16[160,4096]{1,0:T(8,128)(2,1)}, bf16[160,4096]{1,0:T(8,128)(2,1)}, u32[]{:S(2)}, u32[]{:S(2)}) collective-permute-start(bf16[160,4096]{1,0:T(8,128)(2,1)} %slice.316), channel_id=1, source_target_pairs={{0,8},{1,9},{2,10},{3,11},{4,12},{5,13},{6,14},{7,15},{8,16},{9,17... | collective-permute-start | bytes 3932168 | tf_op jit(solution)/shard_map/ppermute | solution.py:24
  126.7 33.1 %collective-permute-start.19 = (bf16[160,4096]{1,0:T(8,128)(2,1)}, bf16[160,4096]{1,0:T(8,128)(2,1)}, u32[]{:S(2)}, u32[]{:S(2)}) collective-permute-start(bf16[160,4096]{1,0:T(8,128)(2,1)} %slice.317), channel_id=1, source_target_pairs={{0,24},{1,25},{2,26},{3,27},{4,28},{5,29},{6,30},{7,31},{8,0},{9,1... | collective-permute-start | bytes 3932168 | tf_op jit(solution)/shard_map/ppermute | solution.py:24
  135.0 4.6 %copy-start.16 = (bf16[4096,448]{0,1:T(8,128)(2,1)S(1)}, bf16[4096,448]{0,1:T(8,128)(2,1)}, u32[]{:S(2)}) copy-start(bf16[4096,448]{0,1:T(8,128)(2,1)} %all-gather.3.cloned.1.call-done) | copy-start | bytes 11010052
  143.7 4.5 %copy-start.18 = (bf16[4096,448]{0,1:T(8,128)(2,1)S(1)}, bf16[4096,448]{0,1:T(8,128)(2,1)}, u32[]{:S(2)}) copy-start(bf16[4096,448]{0,1:T(8,128)(2,1)} %all-gather.5.cloned.1.call-done) | copy-start | bytes 11010052
  156.9 2.1 collective-permute-start.16
  159.0 3.1 %collective-permute-start.17 = (bf16[8,128]{1,0:T(8,128)(2,1)S(1)}, bf16[8,128]{1,0:T(8,128)(2,1)S(1)}, u32[]{:S(2)}, u32[]{:S(2)}) collective-permute-start(bf16[8,128]{1,0:T(8,128)(2,1)S(1)} %collective-permute-done.16), channel_id=1, source_target_pairs={{0,32},{32,0},{64,96},{96,64},{1,33},{33,1},{65,97},{97,65},{2,34}... | collective-permute-start | bytes 6152 | tf_op jit(solution)/shard_map/ppermute | solution.py:38
  177.5 37.4 %collective-permute-start.31 = (f32[2,448,1024]{2,1,0:T(8,128)}, f32[2,448,1024]{2,1,0:T(8,128)}, u32[]{:S(2)}, u32[]{:S(2)}) collective-permute-start(f32[2,448,1024]{2,1,0:T(8,128)} %get-tuple-element.102), channel_id=1, source_target_pairs={{0,32},{32,0},{64,96},{96,64},{1,33},{33,1},{65,97},{97,65},{2,34}... | collective-permute-start | bytes 11010056 | tf_op jit(solution)/shard_map/ppermute | solution.py:38
  177.5 42.4 %collective-permute-start.30 = (f32[2,448,1024]{2,1,0:T(8,128)}, f32[2,448,1024]{2,1,0:T(8,128)}, u32[]{:S(2)}, u32[]{:S(2)}) collective-permute-start(f32[2,448,1024]{2,1,0:T(8,128)} %get-tuple-element.99), channel_id=1, source_target_pairs={{0,32},{32,0},{64,96},{96,64},{1,33},{33,1},{65,97},{97,65},{2,34}... | collective-permute-start | bytes 11010056 | tf_op jit(solution)/shard_map/ppermute | solution.py:38
  179.8 13.0 %copy-start.19 = (s32[4]{0:T(128)S(1)}, s32[4]{0:T(128)}, u32[]{:S(2)}) copy-start(s32[4]{0:T(128)} %param.26) | copy-start | bytes 52
  179.8 64.6 %copy-start.3 = (bf16[2,1024,448]{1,2,0:T(8,128)(2,1)S(1)}, bf16[2,1024,448]{1,2,0:T(8,128)(2,1)}, u32[]{:S(2)}) copy-start(bf16[2,1024,448]{1,2,0:T(8,128)(2,1)} %param.27) | copy-start | bytes 5505028
  190.3 5.2 %collective-permute-start.20 = (f32[8,128]{1,0:T(8,128)S(1)}, f32[8,128]{1,0:T(8,128)S(1)}, u32[]{:S(2)}, u32[]{:S(2)}) collective-permute-start(f32[8,128]{1,0:T(8,128)S(1)} %broadcast_in_dim.9), channel_id=1, source_target_pairs={{0,1},{1,0},{2,3},{3,2},{4,5},{5,4},{6,7},{7,6},{8,9},{9,8},{10,11... | collective-permute-start | bytes 12296 | tf_op jit(solution)/shard_map/ppermute | solution.py:28
  192.5 1.2 collective-permute-start.21
  192.5 3.0 %collective-permute-start.22 = (f32[8,128]{1,0:T(8,128)S(1)}, f32[8,128]{1,0:T(8,128)S(1)}, u32[]{:S(2)}, u32[]{:S(2)}) collective-permute-start(f32[8,128]{1,0:T(8,128)S(1)} %broadcast_in_dim.9), channel_id=1, source_target_pairs={{0,33},{1,32},{2,35},{3,34},{4,37},{5,36},{6,39},{7,38},{8,41},{9,... | collective-permute-start | bytes 12296 | tf_op jit(solution)/shard_map/ppermute | solution.py:34
  196.2 6.0 %collective-permute-start.23 = (f32[16,128]{1,0:T(8,128)S(1)}, f32[16,128]{1,0:T(8,128)S(1)}, u32[]{:S(2)}, u32[]{:S(2)}) collective-permute-start(f32[16,128]{1,0:T(8,128)S(1)} %pad_maximum_fusion.3), channel_id=1, source_target_pairs={{0,8},{1,9},{2,10},{3,11},{4,12},{5,13},{6,14},{7,15},{8,0},{9,1},... | collective-permute-start | bytes 24584 | tf_op jit(solution)/shard_map/ppermute | solution.py:28
  196.7 5.6 %collective-permute-start.24 = (f32[16,128]{1,0:T(8,128)S(1)}, f32[16,128]{1,0:T(8,128)S(1)}, u32[]{:S(2)}, u32[]{:S(2)}) collective-permute-start(f32[16,128]{1,0:T(8,128)S(1)} %pad_maximum_fusion.3), channel_id=1, source_target_pairs={{0,16},{1,17},{2,18},{3,19},{4,20},{5,21},{6,22},{7,23},{8,24},{9,... | collective-permute-start | bytes 24584 | tf_op jit(solution)/shard_map/ppermute | solution.py:28
  199.4 4.9 %collective-permute-start.25 = (f32[16,128]{1,0:T(8,128)S(1)}, f32[16,128]{1,0:T(8,128)S(1)}, u32[]{:S(2)}, u32[]{:S(2)}) collective-permute-start(f32[16,128]{1,0:T(8,128)S(1)} %pad_maximum_fusion.3), channel_id=1, source_target_pairs={{0,24},{1,25},{2,26},{3,27},{4,28},{5,29},{6,30},{7,31},{8,16},{9,... | collective-permute-start | bytes 24584 | tf_op jit(solution)/shard_map/ppermute | solution.py:28
  204.2 6.2 %collective-permute-start.26 = (f32[16,128]{1,0:T(8,128)S(1)}, f32[16,128]{1,0:T(8,128)S(1)}, u32[]{:S(2)}, u32[]{:S(2)}) collective-permute-start(f32[16,128]{1,0:T(8,128)S(1)} %add_add_fusion), channel_id=1, source_target_pairs={{0,2},{1,3},{2,0},{3,1},{4,6},{5,7},{6,4},{7,5},{8,10},{9,11},{10,... | collective-permute-start | bytes 24584 | tf_op jit(solution)/shard_map/ppermute | solution.py:28
  204.2 6.2 %collective-permute-start.27 = (f32[16,128]{1,0:T(8,128)S(1)}, f32[16,128]{1,0:T(8,128)S(1)}, u32[]{:S(2)}, u32[]{:S(2)}) collective-permute-start(f32[16,128]{1,0:T(8,128)S(1)} %add_add_fusion), channel_id=1, source_target_pairs={{0,4},{1,5},{2,6},{3,7},{4,0},{5,1},{6,2},{7,3},{8,12},{9,13},{10,... | collective-permute-start | bytes 24584 | tf_op jit(solution)/shard_map/ppermute | solution.py:28
  205.8 4.9 %collective-permute-start.28 = (f32[16,128]{1,0:T(8,128)S(1)}, f32[16,128]{1,0:T(8,128)S(1)}, u32[]{:S(2)}, u32[]{:S(2)}) collective-permute-start(f32[16,128]{1,0:T(8,128)S(1)} %add_add_fusion), channel_id=1, source_target_pairs={{0,6},{1,7},{2,4},{3,5},{4,2},{5,3},{6,0},{7,1},{8,14},{9,15},{10,... | collective-permute-start | bytes 24584 | tf_op jit(solution)/shard_map/ppermute | solution.py:28
  210.4 9.5 %copy-start.2 = (f32[2,448,1024]{2,1,0:T(8,128)S(1)}, f32[2,448,1024]{2,1,0:T(8,128)}, u32[]{:S(2)}) copy-start(f32[2,448,1024]{2,1,0:T(8,128)} %get-tuple-element.98.keep) | copy-start | bytes 11010052
  211.3 16.0 %collective-permute-start.29 = (f32[8,128]{1,0:T(8,128)S(1)}, f32[8,128]{1,0:T(8,128)S(1)}, u32[]{:S(2)}, u32[]{:S(2)}) collective-permute-start(f32[8,128]{1,0:T(8,128)S(1)} %fusion.18), channel_id=1, source_target_pairs={{0,64},{32,96},{64,0},{96,32},{1,65},{33,97},{65,1},{97,33},{2,66}... | collective-permute-start | bytes 12296 | tf_op jit(solution)/shard_map/ppermute | solution.py:42
  219.3 24.9 %collective-permute-start.32 = (f16[448,1024]{1,0:T(8,128)(2,1)S(1)}, f16[448,1024]{1,0:T(8,128)(2,1)S(1)}, u32[]{:S(2)}, u32[]{:S(2)}) collective-permute-start(f16[448,1024]{1,0:T(8,128)(2,1)S(1)} %fusion.6), channel_id=1, source_target_pairs={{0,64},{32,96},{64,0},{96,32},{1,65},{33,97},{65,1},{97,33},{2,66}... | collective-permute-start | bytes 2752520 | tf_op jit(solution)/shard_map/ppermute | solution.py:42
  219.9 24.5 %copy-start.1 = (f32[2,1024,448]{1,2,0:T(8,128)S(1)}, f32[2,1024,448]{1,2,0:T(8,128)}, u32[]{:S(2)}) copy-start(f32[2,1024,448]{1,2,0:T(8,128)} %param.29) | copy-start | bytes 11010052
  223.2 21.2 %copy-start = (f32[2,1024,448]{1,2,0:T(8,128)S(1)}, f32[2,1024,448]{1,2,0:T(8,128)}, u32[]{:S(2)}) copy-start(f32[2,1024,448]{1,2,0:T(8,128)} %param.28) | copy-start | bytes 11010052
  227.0 1.5 collective-permute-start.33
  228.5 3.2 %collective-permute-start.34 = (f32[8,128]{1,0:T(8,128)S(1)}, f32[8,128]{1,0:T(8,128)S(1)}, u32[]{:S(2)}, u32[]{:S(2)}) collective-permute-start(f32[8,128]{1,0:T(8,128)S(1)} %collective-permute-done.33), channel_id=1, source_target_pairs={{0,32},{32,0},{64,96},{96,64},{1,33},{33,1},{65,97},{97,65},{2,34}... | collective-permute-start | bytes 12296 | tf_op jit(solution)/shard_map/ppermute | solution.py:38
  228.7 28.7 %collective-permute-start.36 = (f16[320,1024]{1,0:T(8,128)(2,1)S(1)}, f16[320,1024]{1,0:T(8,128)(2,1)S(1)}, u32[]{:S(2)}, u32[]{:S(2)}) collective-permute-start(f16[320,1024]{1,0:T(8,128)(2,1)S(1)} %fusion.7), channel_id=1, source_target_pairs={{0,64},{32,96},{64,0},{96,32},{1,65},{33,97},{65,1},{97,33},{2,66}... | collective-permute-start | bytes 1966088 | tf_op jit(solution)/shard_map/ppermute | solution.py:42
  253.5 8.9 %collective-permute-start.35 = (f16[128,1024]{1,0:T(8,128)(2,1)S(1)}, f16[128,1024]{1,0:T(8,128)(2,1)S(1)}, u32[]{:S(2)}, u32[]{:S(2)}) collective-permute-start(f16[128,1024]{1,0:T(8,128)(2,1)S(1)} %fusion.34), channel_id=1, source_target_pairs={{0,64},{32,96},{64,0},{96,32},{1,65},{33,97},{65,1},{97,33},{2,66}... | collective-permute-start | bytes 786440 | tf_op jit(solution)/shard_map/ppermute | solution.py:42
  (11 other events, 25.9 us)
Sparse Core Ops, SparseCore 0:
  9.7 38.7 all-gather.2
  50.2 35.3 all-gather.4
